TPU v7x, 32 devices: a whole 2x2x4 slice. The times are simulated.
32 devices in a mesh: fsdp: 16 (over z, y, x), tensor: 2 (over core).
Axes of the slice: x: 2, y: 2, z: 4, core: 2. Of those that a mesh axis runs over, the one named last changes fastest.
Arguments:
- attention_output: bfloat16 [8192, 8192], P('fsdp', 'tensor'), may hold values from -6 to 6
- frozen_weight: bfloat16 [8192, 4096], P('tensor', 'fsdp'), may hold values from -0.397747564 to 0.397747564
- adapter_down: bfloat16 [8192, 64], P('tensor'), may hold values from -0.06629126 to 0.06629126
- adapter_up: bfloat16 [64, 4096], replicated, may hold values from -0.25 to 0.25
- magnitude: float32 [4096], replicated, may hold values from 0.25 to 1
- cotangent: bfloat16 [8192, 4096], P('fsdp', 'tensor'), may hold values from -3 to 3
Outputs:
- layer_out: bfloat16 [8192, 4096], P('fsdp', 'tensor')
- input_gradient: bfloat16 [8192, 8192], P('fsdp', 'tensor')
- down_gradient: float32 [8192, 64], P('tensor')
- d_up: float32 [64, 4096], P(None, 'tensor')
- d_magnitude: float32 [4096], P('tensor')
All inputs are finite; a program needn't handle non-finite values.
Results may differ from a plain program's by a relative error of at most 0.0085.
Values may be sent and summed in bfloat16 or wider, within the bound.
No kernel may reach another device: no remote copies, remote signals or barrier semaphores. Data moves between devices by JAX's collectives and lax.ppermute only.
A program may use at most 192 MiB of HBM per device.

v0:
```python
import functools
import math

import jax
import jax.numpy as jnp
from jax import lax
from jax.experimental import pallas as pl
from jax.experimental.pallas import tpu as pltpu
from jax.sharding import PartitionSpec as P

eps_norm = 1e-06
def flip(value, axis, bit):
    pairs = [(i, i ^ bit) for i in range(lax.axis_size(axis))]
    return lax.ppermute(value, axis, pairs)


def sum_over(value, axis):
    bit = 1
    while bit < lax.axis_size(axis):
        value = value + flip(value, axis, bit)
        bit *= 2
    return value


def arrivals(z, depth):
    found = [("own", 0)]
    for hops in range(1, depth):
        if z - hops >= 0:
            found.append(("up", hops))
        if z + hops < depth:
            found.append(("down", hops))
    return found


def source_plane(z, depth):
    return [z - hops if way == "up" else z + hops for way, hops in arrivals(z, depth)]


def tied(value, *token):
    return lax.optimization_barrier((value, token))[0]


def chosen_by(index, values):
    result = values[0]
    for place, value in enumerate(values):
        if place:
            result = jnp.where(index == place, value, result)
    return result


def nt(a, b):
    return lax.dot_general(a, b, (((1,), (1,)), ((), ())), preferred_element_type=jnp.float32)


def nn(a, b):
    return jnp.dot(a, b, preferred_element_type=jnp.float32)


def tn(a, b):
    return lax.dot_general(a, b, (((0,), (0,)), ((), ())), preferred_element_type=jnp.float32)


no_cost = pl.CostEstimate(flops=0, bytes_accessed=0, transcendentals=0)
in_order = pltpu.CompilerParams(
    dimension_semantics=("arbitrary",), vmem_limit_bytes=24 * 2**20
)


def complete_kernel(parts, *refs):
    refs = list(refs)
    base = refs.pop(0)[...].astype(jnp.float32)
    for _ in range(parts - 1):
        base = base + refs.pop(0)[...].astype(jnp.float32)
    hidden, up, cot, scale, layer, weighted = refs
    pre = base + nn(hidden[...], up[...])
    layer[...] = (pre * scale[...]).astype(jnp.bfloat16)
    weighted[...] = jnp.sum(cot[...].astype(jnp.float32) * pre, axis=0, keepdims=True)


def complete_columns(parts, hidden, up, cot, scale, first, width):
    height, columns = parts[0].shape

    def own(rows):
        return pl.BlockSpec((rows, width), lambda i: (0, i))

    def across(rows):
        return pl.BlockSpec((rows, width), lambda i: (0, first + i))

    return pl.pallas_call(
        functools.partial(complete_kernel, len(parts)),
        grid=(columns // width,),
        in_specs=[own(height)] * len(parts)
        + [pl.BlockSpec(hidden.shape, lambda i: (0, 0))]
        + [across(up.shape[0]), across(height), across(1)],
        out_specs=[own(height), own(1)],
        out_shape=[
            jax.ShapeDtypeStruct((height, columns), jnp.bfloat16),
            jax.ShapeDtypeStruct((1, columns), jnp.float32),
        ],
        compiler_params=in_order,
        cost_estimate=no_cost,
    )(*parts, hidden, up, cot, scale)


def gradient_kernel(count, *refs):
    total = refs[2 * count][...]
    for number in range(count):
        total += nn(refs[number][...], refs[count + number][...])
    refs[-1][...] = total.astype(jnp.bfloat16)


def last_gradient(gradients, weights, before):
    height, depth = before.shape
    lanes = min(depth, 512)
    across = pl.BlockSpec((height, lanes), lambda i: (0, i))
    return pl.pallas_call(
        functools.partial(gradient_kernel, len(weights)),
        grid=(depth // lanes,),
        in_specs=[pl.BlockSpec(value.shape, lambda i: (0, 0)) for value in gradients]
        + [pl.BlockSpec((value.shape[0], lanes), lambda i: (0, i)) for value in weights]
        + [across],
        out_specs=across,
        out_shape=jax.ShapeDtypeStruct(before.shape, jnp.bfloat16),
        compiler_params=in_order,
        cost_estimate=no_cost,
    )(*gradients, *weights, before)


def assemble_kernel(cases, index, *refs):
    out, semaphore = refs[-2], refs[-1]
    for case, copies in enumerate(cases):

        @pl.when(index[0] == case)
        def _(copies=copies):
            started = []
            for number, (source, part, place) in enumerate(copies):
                copy = pltpu.make_async_copy(
                    refs[source].at[part], out.at[place], semaphore.at[number]
                )
                copy.start()
                started.append(copy)
            for copy in started:
                copy.wait()


def assemble(index, cases, arrays, shape):
    size = 2 * math.prod(shape)
    return pl.pallas_call(
        functools.partial(assemble_kernel, cases),
        in_specs=[pl.BlockSpec(memory_space=pltpu.SMEM)]
        + [pl.BlockSpec(memory_space=pl.ANY)] * len(arrays),
        out_specs=pl.BlockSpec(memory_space=pltpu.VMEM),
        out_shape=jax.ShapeDtypeStruct(shape, arrays[0].dtype),
        scratch_shapes=[pltpu.SemaphoreType.DMA((len(cases[0]),))],
        compiler_params=pltpu.CompilerParams(vmem_limit_bytes=2 * size + 4 * 2**20),
        cost_estimate=no_cost,
    )(index.reshape(1), *arrays)


def reordered_kernel(width, places, source, out):
    for place in range(out.shape[1] // width):
        start = pl.multiple_of(places[place] * width, width)
        out[:, place * width : (place + 1) * width] = source[:, pl.ds(start, width)]


def reordered(matrix, places, width):
    shape = (matrix.shape[0], places.shape[0] * width)
    return pl.pallas_call(
        functools.partial(reordered_kernel, width),
        in_specs=[
            pl.BlockSpec(memory_space=pltpu.SMEM),
            pl.BlockSpec(memory_space=pltpu.VMEM),
        ],
        out_specs=pl.BlockSpec(memory_space=pltpu.VMEM),
        out_shape=jax.ShapeDtypeStruct(shape, matrix.dtype),
        compiler_params=pltpu.CompilerParams(vmem_limit_bytes=24 * 2**20),
        cost_estimate=no_cost,
    )(places, matrix)


def on_device(attention_output, frozen_weight, adapter_down, adapter_up, magnitude, cotangent):
    tensor_count = lax.axis_size("tensor")
    tensor_index = lax.axis_index("tensor")
    fsdp_count = lax.axis_size("fsdp")
    fsdp_index = lax.axis_index("fsdp")
    depth = fsdp_count // 4
    x, y, z = fsdp_index % 2, (fsdp_index // 2) % 2, fsdp_index // 4
    tok_rows, in_rows = attention_output.shape
    rank, output_columns = adapter_up.shape
    own_columns = frozen_weight.shape[1]
    block_columns = output_columns // tensor_count
    plane_columns = output_columns // depth
    block_planes = depth // tensor_count
    grad_scale = (tok_rows * fsdp_count) ** (-0.5)
    across_x = [(i, i ^ 1) for i in range(fsdp_count)]
    across_y = [(i, i ^ 2) for i in range(fsdp_count)]
    z_bits = [1 << i for i in range(2, fsdp_count.bit_length() - 1)]
    planes = chosen_by(
        z, [jnp.array(source_plane(i, depth), jnp.int32)[:, None] for i in range(depth)]
    )
    slots = jnp.arange(4, dtype=jnp.int32)
    owner_of = (4 * planes + 2 * (y ^ (slots // 2)) + (x ^ (slots % 2))).reshape(-1)
    positions = chosen_by(
        z,
        [
            jnp.array([source_plane(i, depth).index(p) for p in range(depth)], jnp.int32)[:, None]
            for i in range(depth)
        ],
    )
    slot_of = (4 * positions + 2 * (y ^ (slots // 2)) + (x ^ (slots % 2))).reshape(-1)
    own_owners = fsdp_count // tensor_count
    own_slots = chosen_by(
        tensor_index, [slot_of[i * own_owners : (i + 1) * own_owners] for i in range(tensor_count)]
    )
    block_offset = tensor_index * block_columns

    def own_block(vector):
        return lax.dynamic_slice_in_dim(vector, block_offset, block_columns, vector.ndim - 1)

    up_own = lax.dynamic_slice_in_dim(adapter_up, fsdp_index * own_columns, own_columns, 1)
    merged = frozen_weight.astype(jnp.float32) + nn(adapter_down, up_own)
    square_own = sum_over(jnp.sum(merged * merged, axis=0), "tensor")

    adapter_hidden = sum_over(nn(attention_output, adapter_down), "tensor").astype(jnp.bfloat16)
    cot_slots = reordered(
        lax.all_gather(cotangent, "tensor", axis=1, tiled=True), owner_of, own_columns
    )
    up_slots = reordered(adapter_up, owner_of, own_columns)
    gram = sum_over(tn(adapter_down, adapter_down), "tensor")

    half = in_rows // 2
    here = jnp.zeros((), jnp.int32)
    all_lanes = slice(None)
    lanes = {"c": slice(0, half), "d": slice(half, in_rows)}
    down_t = adapter_down.T

    def side(bit):
        return (fsdp_index // bit) % 2 == 0

    def widen(value, bit, *token):
        other = flip(tied(value, *token), "fsdp", bit)
        return jnp.concatenate(
            [jnp.where(side(bit), value, other), jnp.where(side(bit), other, value)], axis=-1
        )

    def halve(value, bit, *token):
        middle = value.shape[-1] // 2
        low, high = value[..., :middle], value[..., middle:]
        mine = tied(jnp.where(side(bit), high, low).astype(jnp.bfloat16), *token)
        moved = flip(mine, "fsdp", bit)
        return jnp.where(side(bit), low, high) + moved.astype(jnp.float32)

    def add(value, bit, *token):
        value = tied(value.astype(jnp.bfloat16), *token)
        return (value.astype(jnp.float32) + flip(value, "fsdp", bit).astype(jnp.float32)).astype(
            jnp.bfloat16
        )

    held = {(way, 0): frozen_weight.T for way in ("own", "up", "down")}

    def send_z(hops, *before):
        held["up", hops] = lax.ppermute(
            tied(held["up", hops - 1], *before),
            "fsdp",
            [(i, i + 4) for i in range(fsdp_count - 4) if i // 4 >= hops - 1],
        )
        held["down", hops] = lax.ppermute(
            tied(held["down", hops - 1], *before),
            "fsdp",
            [(i, i - 4) for i in range(4, fsdp_count) if i // 4 + hops - 1 < depth],
        )
        return held["up", hops], held["down", hops]

    def own_block_at(position):
        if position == 0:
            return held["own", 0]
        wanted = [arrivals(plane, depth)[position] for plane in range(depth)]
        sources = sorted(set(wanted))
        cases = [[(sources.index(w), all_lanes, all_lanes)] for w in wanted]
        return assemble(z, cases, [held[w] for w in sources], (own_columns, in_rows))

    finished = []
    running = None

    def across_cores(mine):
        return [mine] + [
            lax.ppermute(
                mine, "tensor", [(i, (i + shift) % tensor_count) for i in range(tensor_count)]
            )
            for shift in range(1, tensor_count)
        ]

    class Columns:
        def __init__(self, copies, sources, slots):
            self.slots = slots
            shape = (len(slots) * own_columns, in_rows)
            self.weight = assemble(here, [copies], sources, shape)
            finished.append(self)

        def of(self, matrix):
            parts = [matrix[:, slot * own_columns : (slot + 1) * own_columns] for slot in self.slots]
            return jnp.concatenate(parts, axis=1)

        def forward(self, *token):
            weight = tied(self.weight, *token)
            product = nt(attention_output, weight).astype(jnp.bfloat16)
            self.exchanged = across_cores(product)
            self.cross = nt(down_t, weight)
            return (*self.exchanged, self.cross)

        def complete(self):
            made = complete_columns(
                self.exchanged,
                adapter_hidden,
                self.of(up_slots),
                self.of(cot_slots),
                self.of(scale_slots),
                0,
                own_columns,
            )
            self.layer, self.weighted = made
            return tuple(made)

        def backward(self, *token):
            nonlocal running
            weight = tied(self.weight, *token)
            running = tied(running + nn(self.of(gradient_slots), weight))
            return (running,)

    def near(position):
        sources = [own[position], over_x[position], over_y[position]]
        copies = [
            (i, all_lanes, (slice(i * own_columns, (i + 1) * own_columns), all_lanes))
            for i in range(3)
        ]
        return Columns(copies, sources, [4 * position + i for i in range(3)])

    def far(which):
        copies, sources, slots = [], [], []
        for number, position in enumerate(which):
            for name, (got, part) in zip("cd", ends[position]):
                copies.append(
                    (
                        len(sources),
                        slice(part * own_columns, (part + 1) * own_columns),
                        (slice(number * own_columns, (number + 1) * own_columns), lanes[name]),
                    )
                )
                sources.append(got)
            slots.append(4 * position + 3)
        return Columns(copies, sources, slots)

    def start_far(which, *before):
        halves = []
        for name, came in (("d", over_y), ("c", over_x)):
            sources = [came[position] for position in which]
            copies = [
                (i, (all_lanes, lanes[name]), slice(i * own_columns, (i + 1) * own_columns))
                for i in range(len(which))
            ]
            shape = (len(which) * own_columns, half)
            halves.append(tied(assemble(here, [copies], sources, shape), *before))
        got_d = lax.ppermute(halves[0], "fsdp", across_x)
        got_c = lax.ppermute(halves[1], "fsdp", across_y)
        for number, position in enumerate(which):
            ends[position] = ((got_c, number), (got_d, number))
        return got_c, got_d

    turns = [("near", [position]) for position in range(depth)]
    turns += [("far", list(range(depth - 2))), ("far", [depth - 2]), ("far", [depth - 1])]
    norms_turn = depth - 1
    own, over_x, over_y, ends = {}, {}, {}, {}
    squares = square_own
    token = work = ()
    arrived = []
    waiting = []
    for number, (kind, which) in enumerate(turns):
        before = (token, work)
        token = ()
        work = ()
        if kind == "near":
            position = which[0]
            own[position] = block = tied(own_block_at(position), *before)
            over_x[position] = lax.ppermute(block, "fsdp", across_x)
            over_y[position] = lax.ppermute(block, "fsdp", across_y)
            token += (over_x[position], over_y[position])
            if position + 1 < depth:
                token += send_z(position + 1, *before)
        else:
            token += start_far(which, *before)

        if number < 2:
            squares = widen(squares, (1, 2)[number], *before)
            work += (squares,)
        if number == norms_turn:
            for bit in z_bits:
                squares = widen(squares, bit, *before)
        if number == norms_turn:
            col_norms = jnp.sqrt(squares + eps_norm)
            col_scale = magnitude / col_norms
            scale_slots = reordered(col_scale[None, :], owner_of, own_columns)
            gradient_slots = (cot_slots.astype(jnp.float32) * scale_slots).astype(jnp.bfloat16)
            lowrank_gradient = nt(gradient_slots, up_slots).astype(jnp.bfloat16)
            scale_block = own_block(col_scale)
            grad_block = (cotangent.astype(jnp.float32) * scale_block[None, :]).astype(jnp.bfloat16)
            sums = jnp.concatenate(
                [tn(lowrank_gradient, attention_output), tn(adapter_hidden, grad_block)], axis=1
            )
            running = nn(lowrank_gradient, down_t)
            work += (sums, running)
        if number == norms_turn + 1:
            for bit in z_bits:
                sums = halve(sums, bit, before)
            sums = add(sums, 1)
            work += (sums,)
        if number == norms_turn + 2:
            sums = add(sums, 2, before)
            work += (sums,)
        if number == norms_turn + 3:
            for bit in reversed(z_bits):
                sums = widen(sums, bit, before)

        for columns in arrived:
            work += columns.forward(before)
            waiting.append(columns)
        arrived = [near(which[0]) if kind == "near" else far(which)]
        if number > norms_turn:
            for columns in waiting[: 1 + (number == len(turns) - 1)]:
                work += columns.backward(before) + columns.complete()
            waiting = waiting[1 + (number == len(turns) - 1) :]
    in_sum = sums[:, :in_rows].astype(jnp.float32)
    up_sum = sums[:, in_rows:].astype(jnp.float32)

    for columns in arrived:
        columns.forward(token)
        waiting.append(columns)
    for columns in waiting:
        columns.complete()
    input_gradient = last_gradient(
        [columns.of(gradient_slots) for columns in waiting],
        [columns.weight for columns in waiting],
        running,
    )
    order = [slot for columns in finished for slot in columns.slots]
    place = jnp.array([order.index(slot) for slot in range(fsdp_count)], jnp.int32)

    def joined_columns(parts, places):
        return reordered(jnp.concatenate(parts, axis=1), place[places], own_columns)

    layer_out = joined_columns([columns.layer for columns in finished], own_slots)

    weighted_parts = [columns.weighted for columns in finished]
    weighted_sum = sum_over(joined_columns(weighted_parts, slot_of)[0], "fsdp")
    weighted = weighted_sum / col_norms
    coef = -weighted * magnitude / (col_norms * col_norms)
    scaled_up = (adapter_up.astype(jnp.float32) * coef[None, :]).astype(jnp.bfloat16)
    up_inner = nt(scaled_up, adapter_up)
    scaled_slots = reordered(scaled_up, owner_of, own_columns)
    norm_down = sum(nn(part.of(scaled_slots), part.weight) for part in finished)
    inner_down = lax.dot_general(
        up_inner,
        adapter_down.astype(jnp.float32),
        (((1,), (1,)), ((), ())),
        precision=lax.Precision.HIGHEST,
    )
    down_gradient = ((in_sum + norm_down + inner_down) * grad_scale).T
    crossed = across_cores(jnp.concatenate([columns.cross for columns in finished], axis=1))
    project = joined_columns([sum(crossed[1:], crossed[0])], own_slots) + jnp.dot(
        gram, own_block(adapter_up).astype(jnp.float32), precision=lax.Precision.HIGHEST
    )
    d_up = (up_sum + project * own_block(coef)[None, :]) * grad_scale
    d_magnitude = own_block(weighted) * grad_scale
    return (layer_out, input_gradient, down_gradient, d_up, d_magnitude)


def solution(mesh):
    return jax.shard_map(
        on_device,
        mesh=mesh,
        in_specs=(
            P("fsdp", "tensor"),
            P("tensor", "fsdp"),
            P("tensor", None),
            P(),
            P(),
            P("fsdp", "tensor"),
        ),
        out_specs=(
            P("fsdp", "tensor"),
            P("fsdp", "tensor"),
            P("tensor", None),
            P(None, "tensor"),
            P("tensor"),
        ),
        check_vma=False,
    )
```

profile of v0, /device:TPU:0, one launch (start us, length us, event | category | flops | bytes accessed | tf_op | source)
XLA Modules:
  0.0 411.3 jit_solution(16479929712750584362)
XLA Ops:
  7.2 4.1 %copy.31 = bf16[4096,256]{0,1:T(8,128)(2,1)} copy(bf16[4096,256]{1,0:T(8,128)(2,1)} %param.16) | data formatting | bytes 4194304 | tf_op args[1]
  12.8 6.9 %collective-permute-start.2 = (bf16[256,4096]{1,0:T(8,128)(2,1)}, bf16[256,4096]{1,0:T(8,128)(2,1)}, u32[]{:S(2)}, u32[]{:S(2)}) collective-permute-start(bf16[256,4096]{1,0:T(8,128)(2,1)} %bitcast.1.refs_0_), channel_id=1, source_target_pairs={{0,8},{2,10},{4,12},{6,14},{8,16},{10,18},{12,20},{14,22},{16,24},... | collective-permute-start | bytes 6291464 | tf_op jit(solution)/shard_map/ppermute | solution.py:262
  19.7 2.0 collective-permute-start.1
  23.2 2.5 fusion.9
  30.2 3.9 fusion.66
  36.8 31.7 %collective-permute-done.5 = f32[256]{0:T(256)S(1)} collective-permute-done((f32[256]{0:T(256)S(1)}, f32[256]{0:T(256)S(1)}, u32[]{:S(2)}, u32[]{:S(2)}) %collective-permute-start.5) | collective-permute-done | bytes 1056 | tf_op jit(solution)/shard_map/ppermute | solution.py:14
  74.1 2.1 collective-permute-start.10
  77.4 2.4 shard_map.182
  81.4 3.4 fusion.10.refs_0_
  84.9 33.6 %collective-permute-done.8 = f32[512]{0:T(512)S(1)} collective-permute-done((f32[512]{0:T(512)S(1)}, f32[512]{0:T(512)S(1)}, u32[]{:S(2)}, u32[]{:S(2)}) %collective-permute-start.8) | collective-permute-done | bytes 2080 | tf_op jit(solution)/shard_map/ppermute | solution.py:14
  118.5 2.7 constant_dynamic-update-slice_fusion.18
  122.0 2.9 shard_map.185.refs_0_
  127.6 2.5 collective-permute-start.15
  131.7 4.3 %fusion.11.refs_0_ = bf16[512,768]{1,0:T(8,128)(2,1)} fusion(bf16[768,4096]{1,0:T(8,128)(2,1)S(1)} %shard_map.187, bf16[512,4096]{1,0:T(8,128)(2,1)S(1)} %copy-done.50), kind=kOutput, calls=%fused_computation.28 | convolution fusion | flops 3221618688 | bytes 11272192 | tf_op jit(solution)/shard_map/dot_general | solution.py:52
  136.0 2.2 copy-done.18
  142.7 3.0 shard_map.196
  146.0 2.7 constant_dynamic-update-slice_fusion.17
  148.7 31.0 %collective-permute-done.16.refs_1_ = bf16[256,4096]{1,0:T(8,128)(2,1)} collective-permute-done((bf16[256,4096]{1,0:T(8,128)(2,1)}, bf16[256,4096]{1,0:T(8,128)(2,1)}, u32[]{:S(2)}, u32[]{:S(2)}) %collective-permute-start.16) | collective-permute-done | bytes 2097184 | tf_op jit(solution)/shard_map/ppermute | solution.py:267
  183.5 2.9 shard_map.191
  186.4 3.4 fusion.12.refs_0_
  191.6 2.7 constant_dynamic-update-slice_fusion.16
  198.6 3.1 multiply_convert_fusion
  201.7 3.7 convolution_convert_fusion.7
  205.4 2.0 fusion.58
  210.1 4.7 %fusion.68 = f32[512,4096]{1,0:T(8,128)} fusion(bf16[512,64]{0,1:T(8,128)(2,1)S(1)} %convolution_convert_fusion.7, bf16[4096,64]{0,1:T(8,128)(2,1)S(1)} %copy-done), kind=kOutput, calls=%fused_computation.165 | convolution fusion | flops 268435456 | bytes 8978432 | tf_op jit(solution)/shard_map/dot_general | solution.py:56
  214.8 2.9 shard_map.190
  222.5 4.8 %collective-permute-done.22.refs_2_.refs_0_ = bf16[256,4096]{1,0:T(8,128)(2,1)S(1)} collective-permute-done((bf16[256,4096]{1,0:T(8,128)(2,1)S(1)}, bf16[256,4096]{1,0:T(8,128)(2,1)S(1)}, u32[]{:S(2)}, u32[]{:S(2)}) %collective-permute-start.22) | collective-permute-done | bytes 2097184 | tf_op jit(solution)/shard_map/ppermute | solution.py:385
  228.6 9.2 %shard_map.194 = bf16[768,4096]{1,0:T(8,128)(2,1)S(1)} custom-call(s32[1]{0:T(128)} %constant.186.clone.1.index, bf16[256,4096]{1,0:T(8,128)(2,1)S(1)} %copy-done.17, bf16[256,4096]{1,0:T(8,128)(2,1)S(1)} %collective-permute-done.21.refs_1_.refs_0_, bf16[256,4096]{1,0:T(8,128)(2,1)S(1)} %collective-permute-done.22.refs_2_.refs_0_), custom_call_target="tpu_custom_call" | custom-call | tf_op jit(solution)/shard_map/pallas_call | solution.py:148
  239.1 3.5 fusion.13.refs_0_
  244.7 8.2 %convolution_add_fusion.3 = f32[512,4096]{1,0:T(8,128)} fusion(f32[512,4096]{1,0:T(8,128)} %fusion.68, bf16[768,4096]{1,0:T(8,128)(2,1)S(1)} %bitcast.108, bf16[512,4096]{1,0:T(8,128)(2,1)} %multiply_convert_fusion), kind=kOutput, calls=%fused_computation.6 | convolution fusion | flops 3223322624 | bytes 23855104 | tf_op jit(solution)/shard_map/dot_general | solution.py:56
  255.2 2.7 constant_dynamic-update-slice_fusion.15
  260.0 6.4 %collective-permute-done.27 = bf16[64,1536]{1,0:T(8,128)(2,1)S(1)} collective-permute-done((bf16[64,1536]{1,0:T(8,128)(2,1)S(1)}, bf16[64,1536]{1,0:T(8,128)(2,1)S(1)}, u32[]{:S(2)}, u32[]{:S(2)}) %collective-permute-start.27) | collective-permute-done | bytes 196640 | tf_op jit(solution)/shard_map/ppermute | solution.py:14
  267.0 2.5 shard_map.195
  270.5 24.8 %collective-permute-done.28 = bf16[64,1536]{1,0:T(8,128)(2,1)S(1)} collective-permute-done((bf16[64,1536]{1,0:T(8,128)(2,1)S(1)}, bf16[64,1536]{1,0:T(8,128)(2,1)S(1)}, u32[]{:S(2)}, u32[]{:S(2)}) %collective-permute-start.28) | collective-permute-done | bytes 196640 | tf_op jit(solution)/shard_map/ppermute | solution.py:14
  296.0 1.8 shard_map.198.refs_3_
  299.5 2.4 fusion.14.refs_0_
  304.0 8.0 %convolution_add_fusion.2 = f32[512,4096]{1,0:T(8,128)} fusion(f32[512,4096]{1,0:T(8,128)} %convolution_add_fusion.3, bf16[768,4096]{1,0:T(8,128)(2,1)S(1)} %bitcast.106, bf16[512,4096]{1,0:T(8,128)(2,1)} %multiply_convert_fusion), kind=kOutput, calls=%fused_computation.5 | convolution fusion | flops 3223322624 | bytes 23855104 | tf_op jit(solution)/shard_map/dot_general | solution.py:56
  312.0 2.1 constant_dynamic-update-slice_fusion.14
  316.9 10.7 %collective-permute-done.30.refs_0_ = bf16[256,2048]{1,0:T(8,128)(2,1)S(1)} collective-permute-done((bf16[256,2048]{1,0:T(8,128)(2,1)S(1)}, bf16[256,2048]{1,0:T(8,128)(2,1)S(1)}, u32[]{:S(2)}, u32[]{:S(2)}) %collective-permute-start.30) | collective-permute-done | bytes 1048608 | tf_op jit(solution)/shard_map/ppermute | solution.py:364
  332.9 8.0 %convolution_add_fusion.1 = f32[512,4096]{1,0:T(8,128)} fusion(f32[512,4096]{1,0:T(8,128)} %convolution_add_fusion.2, bf16[768,4096]{1,0:T(8,128)(2,1)S(1)} %shard_map.191, bf16[512,4096]{1,0:T(8,128)(2,1)} %multiply_convert_fusion), kind=kOutput, calls=%fused_computation.4 | convolution fusion | flops 3223322624 | bytes 23855104 | tf_op jit(solution)/shard_map/dot_general | solution.py:56
  340.9 8.0 %convolution_add_fusion.refs_6_ = f32[512,4096]{1,0:T(8,128)} fusion(f32[512,4096]{1,0:T(8,128)} %convolution_add_fusion.1, bf16[768,4096]{1,0:T(8,128)(2,1)S(1)} %shard_map.194, bf16[512,4096]{1,0:T(8,128)(2,1)} %multiply_convert_fusion), kind=kOutput, calls=%fused_computation.3 | convolution fusion | flops 3223322624 | bytes 23855104 | tf_op jit(solution)/shard_map/dot_general | solution.py:56
  350.5 6.6 %collective-permute-done.34.refs_0_ = bf16[256,2048]{1,0:T(8,128)(2,1)S(1)} collective-permute-done((bf16[256,2048]{1,0:T(8,128)(2,1)S(1)}, bf16[256,2048]{1,0:T(8,128)(2,1)S(1)}, u32[]{:S(2)}, u32[]{:S(2)}) %collective-permute-start.34) | collective-permute-done | bytes 1048608 | tf_op jit(solution)/shard_map/ppermute | solution.py:364
  363.2 2.7 collective-permute-done.39
  371.9 2.2 copy-done.4
  374.1 7.7 %shard_map.209 = bf16[512,4096]{1,0:T(8,128)(2,1)} custom-call(bf16[512,512]{1,0:T(8,128)(2,1)S(1)} %pad_maximum_fusion.3.refs_0_, bf16[512,256]{1,0:T(8,128)(2,1)S(1)} %copy-done.23, bf16[512,256]{1,0:T(8,128)(2,1)S(1)} %get-tuple-element.99.refs_2_, bf16[512,4096]{1,0:T(8,128)(2,1)S(1)} %copy-done.4, bf16[256,4096]{1,0:T(8,128)(2,1)S(1)} %shard_map.202.refs_4_, ...), custom_call_target="tpu_custom_call" | custom-call | tf_op jit(solution)/shard_map/pallas_call | solution.py:116
  381.9 3.0 collective-permute-start.42
  385.6 3.9 shard_map.208
  398.4 2.4 multiply_bitcast_fusion
  (341 shorter events, 94.4 us)
Async XLA Ops:
  7.2 128.8 %all-gather.2.cloned.1.call-start = ((), (), s32[]{:S(2)}) async-start(), calls=%async_computation | async-start | bytes 6291456 | tf_op jit(solution)/shard_map/all_gather | solution.py:226
  11.4 57.2 %collective-permute-start.3 = (bf16[256,4096]{1,0:T(8,128)(2,1)}, bf16[256,4096]{1,0:T(8,128)(2,1)}, u32[]{:S(2)}, u32[]{:S(2)}) collective-permute-start(bf16[256,4096]{1,0:T(8,128)(2,1)} %bitcast.1.refs_0_), channel_id=1, source_target_pairs={{8,0},{10,2},{12,4},{14,6},{16,8},{18,10},{20,12},{22,14},{24,16},... | collective-permute-start | bytes 6291464 | tf_op jit(solution)/shard_map/ppermute | solution.py:267
  12.8 56.3 %collective-permute-start.2 = (bf16[256,4096]{1,0:T(8,128)(2,1)}, bf16[256,4096]{1,0:T(8,128)(2,1)}, u32[]{:S(2)}, u32[]{:S(2)}) collective-permute-start(bf16[256,4096]{1,0:T(8,128)(2,1)} %bitcast.1.refs_0_), channel_id=1, source_target_pairs={{0,8},{2,10},{4,12},{6,14},{8,16},{10,18},{12,20},{14,22},{16,24},... | collective-permute-start | bytes 6291464 | tf_op jit(solution)/shard_map/ppermute | solution.py:262
  19.7 51.0 %collective-permute-start.1 = (bf16[256,4096]{1,0:T(8,128)(2,1)}, bf16[256,4096]{1,0:T(8,128)(2,1)S(1)}, u32[]{:S(2)}, u32[]{:S(2)}) collective-permute-start(bf16[256,4096]{1,0:T(8,128)(2,1)} %bitcast.1.refs_0_), channel_id=1, source_target_pairs={{0,4},{2,6},{4,0},{6,2},{8,12},{10,14},{12,8},{14,10},{16,20},{18,... | collective-permute-start | bytes 6291464 | tf_op jit(solution)/shard_map/ppermute | solution.py:385
  21.7 49.1 %collective-permute-start = (bf16[256,4096]{1,0:T(8,128)(2,1)}, bf16[256,4096]{1,0:T(8,128)(2,1)}, u32[]{:S(2)}, u32[]{:S(2)}) collective-permute-start(bf16[256,4096]{1,0:T(8,128)(2,1)} %bitcast.1.refs_0_), channel_id=1, source_target_pairs={{0,2},{2,0},{4,6},{6,4},{8,10},{10,8},{12,14},{14,12},{16,18},{18,... | collective-permute-start | bytes 6291464 | tf_op jit(solution)/shard_map/ppermute | solution.py:384
  25.7 8.5 %collective-permute-start.4 = (f32[256]{0:T(256)S(1)}, f32[256]{0:T(256)S(1)}, u32[]{:S(2)}, u32[]{:S(2)}) collective-permute-start(f32[256]{0:T(256)S(1)} %fusion.9), channel_id=1, source_target_pairs={{0,1},{1,0},{2,3},{3,2},{4,5},{5,4},{6,7},{7,6},{8,9},{9,8},{10,11... | collective-permute-start | bytes 3080 | tf_op jit(solution)/shard_map/ppermute | solution.py:14
  34.2 34.3 %collective-permute-start.5 = (f32[256]{0:T(256)S(1)}, f32[256]{0:T(256)S(1)}, u32[]{:S(2)}, u32[]{:S(2)}) collective-permute-start(f32[256]{0:T(256)S(1)} %add.240), channel_id=1, source_target_pairs={{0,2},{2,0},{4,6},{6,4},{8,10},{10,8},{12,14},{14,12},{16,18},{18,... | collective-permute-start | bytes 3080 | tf_op jit(solution)/shard_map/ppermute | solution.py:14
  36.8 39.4 %copy-start.20 = (bf16[64,4096]{1,0:T(8,128)(2,1)S(1)}, bf16[64,4096]{1,0:T(8,128)(2,1)}, u32[]{:S(2)}) copy-start(bf16[64,4096]{1,0:T(8,128)(2,1)} %source.1) | copy-start | bytes 1572868
  68.5 5.6 %collective-permute-start.44 = (f32[64,64]{1,0:T(8,128)S(1)}, f32[64,64]{1,0:T(8,128)S(1)}, u32[]{:S(2)}, u32[]{:S(2)}) collective-permute-start(f32[64,64]{1,0:T(8,128)S(1)} %fusion.70), channel_id=1, source_target_pairs={{0,1},{1,0},{2,3},{3,2},{4,5},{5,4},{6,7},{7,6},{8,9},{9,8},{10,11... | collective-permute-start | bytes 49160 | tf_op jit(solution)/shard_map/ppermute | solution.py:14
  68.6 11.2 %collective-permute-start.7 = (f32[512,64]{1,0:T(8,128)S(1)}, f32[512,64]{1,0:T(8,128)S(1)}, u32[]{:S(2)}, u32[]{:S(2)}) collective-permute-start(f32[512,64]{1,0:T(8,128)S(1)} %fusion.66), channel_id=1, source_target_pairs={{0,1},{1,0},{2,3},{3,2},{4,5},{5,4},{6,7},{7,6},{8,9},{9,8},{10,11... | collective-permute-start | bytes 393224 | tf_op jit(solution)/shard_map/ppermute | solution.py:14
  70.8 54.2 %collective-permute-start.12 = (bf16[256,4096]{1,0:T(8,128)(2,1)S(1)}, bf16[256,4096]{1,0:T(8,128)(2,1)S(1)}, u32[]{:S(2)}, u32[]{:S(2)}) collective-permute-start(bf16[256,4096]{1,0:T(8,128)(2,1)S(1)} %shard_map.186.refs_0_), channel_id=1, source_target_pairs={{0,4},{2,6},{4,0},{6,2},{8,12},{10,14},{12,8},{14,10},{16,20},{18,... | collective-permute-start | bytes 6291464 | tf_op jit(solution)/shard_map/ppermute | solution.py:385
  71.2 53.8 %collective-permute-start.11 = (bf16[256,4096]{1,0:T(8,128)(2,1)S(1)}, bf16[256,4096]{1,0:T(8,128)(2,1)S(1)}, u32[]{:S(2)}, u32[]{:S(2)}) collective-permute-start(bf16[256,4096]{1,0:T(8,128)(2,1)S(1)} %shard_map.186.refs_0_), channel_id=1, source_target_pairs={{0,2},{2,0},{4,6},{6,4},{8,10},{10,8},{12,14},{14,12},{16,18},{18,... | collective-permute-start | bytes 6291464 | tf_op jit(solution)/shard_map/ppermute | solution.py:384
  72.8 49.2 %collective-permute-start.9 = (bf16[256,4096]{1,0:T(8,128)(2,1)}, bf16[256,4096]{1,0:T(8,128)(2,1)}, u32[]{:S(2)}, u32[]{:S(2)}) collective-permute-start(bf16[256,4096]{1,0:T(8,128)(2,1)} %collective-permute-done.3.refs_0_), channel_id=1, source_target_pairs={{8,0},{10,2},{12,4},{14,6},{16,8},{18,10},{20,12},{22,14},{9,1},{1... | collective-permute-start | bytes 6291464 | tf_op jit(solution)/shard_map/ppermute | solution.py:267
  74.1 47.9 %collective-permute-start.10 = (bf16[256,4096]{1,0:T(8,128)(2,1)}, bf16[256,4096]{1,0:T(8,128)(2,1)}, u32[]{:S(2)}, u32[]{:S(2)}) collective-permute-start(bf16[256,4096]{1,0:T(8,128)(2,1)} %collective-permute-done.2.refs_1_), channel_id=1, source_target_pairs={{8,16},{10,18},{12,20},{14,22},{16,24},{18,26},{20,28},{22,30},{9,... | collective-permute-start | bytes 6291464 | tf_op jit(solution)/shard_map/ppermute | solution.py:262
  79.8 38.6 %collective-permute-start.8 = (f32[512]{0:T(512)S(1)}, f32[512]{0:T(512)S(1)}, u32[]{:S(2)}, u32[]{:S(2)}) collective-permute-start(f32[512]{0:T(512)S(1)} %pad_maximum_fusion.8), channel_id=1, source_target_pairs={{0,4},{2,6},{4,0},{6,2},{8,12},{10,14},{12,8},{14,10},{16,20},{18,... | collective-permute-start | bytes 6152 | tf_op jit(solution)/shard_map/ppermute | solution.py:14
  84.8 40.1 %copy-start.34 = (bf16[512,768]{1,0:T(8,128)(2,1)}, bf16[512,768]{1,0:T(8,128)(2,1)S(1)}, u32[]{:S(2)}) copy-start(bf16[512,768]{1,0:T(8,128)(2,1)S(1)} %fusion.10.refs_0_) | copy-start | bytes 2359300
  118.4 6.5 %collective-permute-start.6 = (bf16[512,768]{1,0:T(8,128)(2,1)S(1)}, bf16[512,768]{1,0:T(8,128)(2,1)S(1)}, u32[]{:S(2)}, u32[]{:S(2)}) collective-permute-start(bf16[512,768]{1,0:T(8,128)(2,1)S(1)} %fusion.10.refs_0_), channel_id=1, source_target_pairs={{0,1},{1,0},{2,3},{3,2},{4,5},{5,4},{6,7},{7,6},{8,9},{9,8},{10,11... | collective-permute-start | bytes 2359304 | tf_op jit(solution)/shard_map/ppermute | solution.py:287
  125.0 56.4 %collective-permute-start.14 = (bf16[256,4096]{1,0:T(8,128)(2,1)}, bf16[256,4096]{1,0:T(8,128)(2,1)}, u32[]{:S(2)}, u32[]{:S(2)}) collective-permute-start(bf16[256,4096]{1,0:T(8,128)(2,1)} %shard_map.185.refs_0_), channel_id=1, source_target_pairs={{0,4},{2,6},{4,0},{6,2},{8,12},{10,14},{12,8},{14,10},{16,20},{18,... | collective-permute-start | bytes 6291464 | tf_op jit(solution)/shard_map/ppermute | solution.py:385
  126.6 54.8 %collective-permute-start.13 = (bf16[256,4096]{1,0:T(8,128)(2,1)}, bf16[256,4096]{1,0:T(8,128)(2,1)}, u32[]{:S(2)}, u32[]{:S(2)}) collective-permute-start(bf16[256,4096]{1,0:T(8,128)(2,1)} %shard_map.185.refs_0_), channel_id=1, source_target_pairs={{0,2},{2,0},{4,6},{6,4},{8,10},{10,8},{12,14},{14,12},{16,18},{18,... | collective-permute-start | bytes 6291464 | tf_op jit(solution)/shard_map/ppermute | solution.py:384
  127.6 21.1 %collective-permute-start.15 = (bf16[256,4096]{1,0:T(8,128)(2,1)}, bf16[256,4096]{1,0:T(8,128)(2,1)}, u32[]{:S(2)}, u32[]{:S(2)}) collective-permute-start(bf16[256,4096]{1,0:T(8,128)(2,1)} %collective-permute-done.10.refs_2_), channel_id=1, source_target_pairs={{16,24},{18,26},{20,28},{22,30},{17,25},{19,27},{21,29},{23,31}} | collective-permute-start | bytes 6291464 | tf_op jit(solution)/shard_map/ppermute | solution.py:262
  130.1 49.6 %collective-permute-start.16 = (bf16[256,4096]{1,0:T(8,128)(2,1)}, bf16[256,4096]{1,0:T(8,128)(2,1)}, u32[]{:S(2)}, u32[]{:S(2)}) collective-permute-start(bf16[256,4096]{1,0:T(8,128)(2,1)} %collective-permute-done.9.refs_1_.refs_0_), channel_id=1, source_target_pairs={{8,0},{10,2},{12,4},{14,6},{9,1},{11,3},{13,5},{15,7}} | collective-permute-start | bytes 6291464 | tf_op jit(solution)/shard_map/ppermute | solution.py:267
  136.0 45.4 %collective-permute-start.17 = (bf16[512,768]{1,0:T(8,128)(2,1)}, bf16[512,768]{1,0:T(8,128)(2,1)}, u32[]{:S(2)}, u32[]{:S(2)}) collective-permute-start(bf16[512,768]{1,0:T(8,128)(2,1)} %fusion.11.refs_0_), channel_id=1, source_target_pairs={{0,1},{1,0},{2,3},{3,2},{4,5},{5,4},{6,7},{7,6},{8,9},{9,8},{10,11... | collective-permute-start | bytes 2359304 | tf_op jit(solution)/shard_map/ppermute | solution.py:287
  181.4 45.9 %collective-permute-start.22 = (bf16[256,4096]{1,0:T(8,128)(2,1)S(1)}, bf16[256,4096]{1,0:T(8,128)(2,1)S(1)}, u32[]{:S(2)}, u32[]{:S(2)}) collective-permute-start(bf16[256,4096]{1,0:T(8,128)(2,1)S(1)} %shard_map.193.refs_0_), channel_id=1, source_target_pairs={{0,4},{2,6},{4,0},{6,2},{8,12},{10,14},{12,8},{14,10},{16,20},{18,... | collective-permute-start | bytes 6291464 | tf_op jit(solution)/shard_map/ppermute | solution.py:385
  182.8 45.8 %collective-permute-start.21 = (bf16[256,4096]{1,0:T(8,128)(2,1)S(1)}, bf16[256,4096]{1,0:T(8,128)(2,1)S(1)}, u32[]{:S(2)}, u32[]{:S(2)}) collective-permute-start(bf16[256,4096]{1,0:T(8,128)(2,1)S(1)} %shard_map.193.refs_0_), channel_id=1, source_target_pairs={{0,2},{2,0},{4,6},{6,4},{8,10},{10,8},{12,14},{14,12},{16,18},{18,... | collective-permute-start | bytes 6291464 | tf_op jit(solution)/shard_map/ppermute | solution.py:384
  183.5 6.4 %collective-permute-start.18 = (f32[1024]{0:T(1024)S(1)}, f32[1024]{0:T(1024)S(1)}, u32[]{:S(2)}, u32[]{:S(2)}) collective-permute-start(f32[1024]{0:T(1024)S(1)} %copy-done.65), channel_id=1, source_target_pairs={{0,8},{2,10},{4,12},{6,14},{8,0},{10,2},{12,4},{14,6},{16,24},{18,... | collective-permute-start | bytes 12296 | tf_op jit(solution)/shard_map/ppermute | solution.py:14
  189.9 7.4 %collective-permute-start.19 = (f32[2048]{0:T(1024)S(1)}, f32[2048]{0:T(1024)S(1)}, u32[]{:S(2)}, u32[]{:S(2)}) collective-permute-start(f32[2048]{0:T(1024)S(1)} %pad_maximum_fusion.6), channel_id=1, source_target_pairs={{0,16},{2,18},{4,20},{6,22},{8,24},{10,26},{12,28},{14,30},{16,0},... | collective-permute-start | bytes 24584 | tf_op jit(solution)/shard_map/ppermute | solution.py:14
  194.4 26.1 %collective-permute-start.20 = (bf16[512,768]{1,0:T(8,128)(2,1)S(1)}, bf16[512,768]{1,0:T(8,128)(2,1)S(1)}, u32[]{:S(2)}, u32[]{:S(2)}) collective-permute-start(bf16[512,768]{1,0:T(8,128)(2,1)S(1)} %fusion.12.refs_0_), channel_id=1, source_target_pairs={{0,1},{1,0},{2,3},{3,2},{4,5},{5,4},{6,7},{7,6},{8,9},{9,8},{10,11... | collective-permute-start | bytes 2359304 | tf_op jit(solution)/shard_map/ppermute | solution.py:287
  239.1 13.7 %collective-permute-start.26 = (bf16[64,3072]{1,0:T(8,128)(2,1)}, bf16[64,3072]{1,0:T(8,128)(2,1)}, u32[]{:S(2)}, u32[]{:S(2)}) collective-permute-start(bf16[64,3072]{1,0:T(8,128)(2,1)} %select_convert_fusion), channel_id=1, source_target_pairs={{0,8},{2,10},{4,12},{6,14},{8,0},{10,2},{12,4},{14,6},{16,24},{18,... | collective-permute-start | bytes 1179656 | tf_op jit(solution)/shard_map/ppermute | solution.py:14
  242.6 24.4 %collective-permute-start.23 = (bf16[512,768]{1,0:T(8,128)(2,1)S(1)}, bf16[512,768]{1,0:T(8,128)(2,1)}, u32[]{:S(2)}, u32[]{:S(2)}) collective-permute-start(bf16[512,768]{1,0:T(8,128)(2,1)S(1)} %fusion.13.refs_0_), channel_id=1, source_target_pairs={{0,1},{1,0},{2,3},{3,2},{4,5},{5,4},{6,7},{7,6},{8,9},{9,8},{10,11... | collective-permute-start | bytes 2359304 | tf_op jit(solution)/shard_map/ppermute | solution.py:287
  242.7 53.4 %collective-permute-start.24 = (bf16[512,2048]{1,0:T(8,128)(2,1)}, bf16[512,2048]{1,0:T(8,128)(2,1)S(1)}, u32[]{:S(2)}, u32[]{:S(2)}) collective-permute-start(bf16[512,2048]{1,0:T(8,128)(2,1)} %shard_map.196), channel_id=1, source_target_pairs={{0,4},{2,6},{4,0},{6,2},{8,12},{10,14},{12,8},{14,10},{16,20},{18,... | collective-permute-start | bytes 6291464 | tf_op jit(solution)/shard_map/ppermute | solution.py:364
  243.2 52.8 %collective-permute-start.25 = (bf16[512,2048]{1,0:T(8,128)(2,1)}, bf16[512,2048]{1,0:T(8,128)(2,1)}, u32[]{:S(2)}, u32[]{:S(2)}) collective-permute-start(bf16[512,2048]{1,0:T(8,128)(2,1)} %shard_map.197), channel_id=1, source_target_pairs={{0,2},{2,0},{4,6},{6,4},{8,10},{10,8},{12,14},{14,12},{16,18},{18,... | collective-permute-start | bytes 6291464 | tf_op jit(solution)/shard_map/ppermute | solution.py:363
  254.5 11.9 %collective-permute-start.27 = (bf16[64,1536]{1,0:T(8,128)(2,1)S(1)}, bf16[64,1536]{1,0:T(8,128)(2,1)S(1)}, u32[]{:S(2)}, u32[]{:S(2)}) collective-permute-start(bf16[64,1536]{1,0:T(8,128)(2,1)S(1)} %select_convert_fusion.1), channel_id=1, source_target_pairs={{0,16},{2,18},{4,20},{6,22},{8,24},{10,26},{12,28},{14,30},{16,0},... | collective-permute-start | bytes 589832 | tf_op jit(solution)/shard_map/ppermute | solution.py:14
  266.4 28.9 %collective-permute-start.28 = (bf16[64,1536]{1,0:T(8,128)(2,1)S(1)}, bf16[64,1536]{1,0:T(8,128)(2,1)S(1)}, u32[]{:S(2)}, u32[]{:S(2)}) collective-permute-start(bf16[64,1536]{1,0:T(8,128)(2,1)S(1)} %add_convert_fusion.2), channel_id=1, source_target_pairs={{0,2},{2,0},{4,6},{6,4},{8,10},{10,8},{12,14},{14,12},{16,18},{18,... | collective-permute-start | bytes 589832 | tf_op jit(solution)/shard_map/ppermute | solution.py:14
  297.9 16.2 %collective-permute-start.32 = (bf16[64,1536]{1,0:T(8,128)(2,1)}, bf16[64,1536]{1,0:T(8,128)(2,1)S(1)}, u32[]{:S(2)}, u32[]{:S(2)}) collective-permute-start(bf16[64,1536]{1,0:T(8,128)(2,1)} %add_convert_fusion.1), channel_id=1, source_target_pairs={{0,4},{2,6},{4,0},{6,2},{8,12},{10,14},{12,8},{14,10},{16,20},{18,... | collective-permute-start | bytes 589832 | tf_op jit(solution)/shard_map/ppermute | solution.py:14
  301.9 13.3 %collective-permute-start.29 = (bf16[512,512]{1,0:T(8,128)(2,1)S(1)}, bf16[512,512]{1,0:T(8,128)(2,1)S(1)}, u32[]{:S(2)}, u32[]{:S(2)}) collective-permute-start(bf16[512,512]{1,0:T(8,128)(2,1)S(1)} %fusion.14.refs_0_), channel_id=1, source_target_pairs={{0,1},{1,0},{2,3},{3,2},{4,5},{5,4},{6,7},{7,6},{8,9},{9,8},{10,11... | collective-permute-start | bytes 1572872 | tf_op jit(solution)/shard_map/ppermute | solution.py:287
  302.0 25.6 %collective-permute-start.30 = (bf16[256,2048]{1,0:T(8,128)(2,1)S(1)}, bf16[256,2048]{1,0:T(8,128)(2,1)S(1)}, u32[]{:S(2)}, u32[]{:S(2)}) collective-permute-start(bf16[256,2048]{1,0:T(8,128)(2,1)S(1)} %copy-done.27), channel_id=1, source_target_pairs={{0,4},{2,6},{4,0},{6,2},{8,12},{10,14},{12,8},{14,10},{16,20},{18,... | collective-permute-start | bytes 3145736 | tf_op jit(solution)/shard_map/ppermute | solution.py:364
  303.1 25.2 %collective-permute-start.31 = (bf16[256,2048]{1,0:T(8,128)(2,1)S(1)}, bf16[256,2048]{1,0:T(8,128)(2,1)S(1)}, u32[]{:S(2)}, u32[]{:S(2)}) collective-permute-start(bf16[256,2048]{1,0:T(8,128)(2,1)S(1)} %copy-done.25), channel_id=1, source_target_pairs={{0,2},{2,0},{4,6},{6,4},{8,10},{10,8},{12,14},{14,12},{16,18},{18,... | collective-permute-start | bytes 3145736 | tf_op jit(solution)/shard_map/ppermute | solution.py:363
  328.7 20.3 %collective-permute-start.37 = (bf16[64,1536]{1,0:T(8,128)(2,1)S(1)}, bf16[64,1536]{1,0:T(8,128)(2,1)S(1)}, u32[]{:S(2)}, u32[]{:S(2)}) collective-permute-start(bf16[64,1536]{1,0:T(8,128)(2,1)S(1)} %add_convert_fusion), channel_id=1, source_target_pairs={{0,16},{2,18},{4,20},{6,22},{8,24},{10,26},{12,28},{14,30},{16,0},... | collective-permute-start | bytes 589832 | tf_op jit(solution)/shard_map/ppermute | solution.py:14
  331.4 29.5 %collective-permute-start.33 = (bf16[512,256]{1,0:T(8,128)(2,1)S(1)}, bf16[512,256]{1,0:T(8,128)(2,1)S(1)}, u32[]{:S(2)}, u32[]{:S(2)}) collective-permute-start(bf16[512,256]{1,0:T(8,128)(2,1)S(1)} %fusion.15.refs_0_), channel_id=1, source_target_pairs={{0,1},{1,0},{2,3},{3,2},{4,5},{5,4},{6,7},{7,6},{8,9},{9,8},{10,11... | collective-permute-start | bytes 786440 | tf_op jit(solution)/shard_map/ppermute | solution.py:287
  331.5 25.6 %collective-permute-start.34 = (bf16[256,2048]{1,0:T(8,128)(2,1)S(1)}, bf16[256,2048]{1,0:T(8,128)(2,1)S(1)}, u32[]{:S(2)}, u32[]{:S(2)}) collective-permute-start(bf16[256,2048]{1,0:T(8,128)(2,1)S(1)} %copy-done.31), channel_id=1, source_target_pairs={{0,4},{2,6},{4,0},{6,2},{8,12},{10,14},{12,8},{14,10},{16,20},{18,... | collective-permute-start | bytes 3145736 | tf_op jit(solution)/shard_map/ppermute | solution.py:364
  332.6 25.2 %collective-permute-start.35 = (bf16[256,2048]{1,0:T(8,128)(2,1)S(1)}, bf16[256,2048]{1,0:T(8,128)(2,1)S(1)}, u32[]{:S(2)}, u32[]{:S(2)}) collective-permute-start(bf16[256,2048]{1,0:T(8,128)(2,1)S(1)} %copy-done.29), channel_id=1, source_target_pairs={{0,2},{2,0},{4,6},{6,4},{8,10},{10,8},{12,14},{14,12},{16,18},{18,... | collective-permute-start | bytes 3145736 | tf_op jit(solution)/shard_map/ppermute | solution.py:363
  349.0 17.9 %collective-permute-start.38 = (bf16[64,3072]{1,0:T(8,128)(2,1)S(1)}, bf16[64,3072]{1,0:T(8,128)(2,1)S(1)}, u32[]{:S(2)}, u32[]{:S(2)}) collective-permute-start(bf16[64,3072]{1,0:T(8,128)(2,1)S(1)} %pad_maximum_fusion.4), channel_id=1, source_target_pairs={{0,8},{2,10},{4,12},{6,14},{8,0},{10,2},{12,4},{14,6},{16,24},{18,... | collective-permute-start | bytes 1179656 | tf_op jit(solution)/shard_map/ppermute | solution.py:14
  359.5 1.8 collective-permute-start.36
  362.1 3.8 collective-permute-start.39
  365.9 3.7 collective-permute-start.40
  369.6 12.2 %collective-permute-start.41 = (f32[4096]{0:T(1024)S(1)}, f32[4096]{0:T(1024)S(1)}, u32[]{:S(2)}, u32[]{:S(2)}) collective-permute-start(f32[4096]{0:T(1024)S(1)} %add.262), channel_id=1, source_target_pairs={{0,8},{2,10},{4,12},{6,14},{8,0},{10,2},{12,4},{14,6},{16,24},{18,... | collective-permute-start | bytes 49160 | tf_op jit(solution)/shard_map/ppermute | solution.py:14
  371.9 29.0 %collective-permute-start.43 = (f32[64,4096]{1,0:T(8,128)}, f32[64,4096]{1,0:T(8,128)}, u32[]{:S(2)}, u32[]{:S(2)}) collective-permute-start(f32[64,4096]{1,0:T(8,128)} %fusion.17), channel_id=1, source_target_pairs={{0,1},{1,0},{2,3},{3,2},{4,5},{5,4},{6,7},{7,6},{8,9},{9,8},{10,11... | collective-permute-start | bytes 3145736 | tf_op jit(solution)/shard_map/ppermute | solution.py:287
  381.9 7.6 %collective-permute-start.42 = (f32[4096]{0:T(1024)S(1)}, f32[4096]{0:T(1024)S(1)}, u32[]{:S(2)}, u32[]{:S(2)}) collective-permute-start(f32[4096]{0:T(1024)S(1)} %add.263), channel_id=1, source_target_pairs={{0,16},{2,18},{4,20},{6,22},{8,24},{10,26},{12,28},{14,30},{16,0},... | collective-permute-start | bytes 49160 | tf_op jit(solution)/shard_map/ppermute | solution.py:14
  (76 other events, 512.8 us)
Sparse Core Ops, SparseCore 0:
  23.3 12.0 all-gather.1
where the time goes:
time: 419 us; the launch traced here: 411 us
  waiting for transfers between devices  157 us (37%)
  matrix products  94.1 us (22%)
  Pallas kernels  55.3 us (13%)
  starting transfers between devices  46.8 us (11%)
  local copies, waits for them, and re-layouts  28 us (7%)
  between operations  16.1 us (4%)
  other arithmetic  14.2 us (3%)
    ppermute x17, waiting for transfers between devices, flip(): return lax.ppermute(value, axis, pairs)  101 us
    dot_general x14, matrix products, nn(): return jnp.dot(a, b, preferred_element_type=jnp.float32)  51.1 us
    dot_general x16, matrix products, nt(): lax.dot_general(a, b, (((1,), (1,)), ((), ())), preferred_element_type=jn...  39.5 us
    ppermute x3, waiting for transfers between devices, send_z(): lax.ppermute(tied(held['down', hops - 1], *before), 'fsdp', [(i, i - 4) f...  31.2 us
    pallas_call x16, Pallas kernels, assemble(): pl.pallas_call(functools.partial(assemble_kernel, cases), in_specs=[pl.Bl...  31 us
    unnamed x169, local copies, waits for them, and re-layouts  20.4 us
    ppermute x3, waiting for transfers between devices, start_far(): got_c = lax.ppermute(halves[1], 'fsdp', across_y)  17.2 us
    ppermute x17, starting transfers between devices, flip(): return lax.ppermute(value, axis, pairs)  15.6 us
  transfers between devices with their start and end apart: 46, of which 14 were waited for; matrix products, arithmetic and copies ran while one was open for 29% of the time, Pallas kernels for 11%

commit v1 on v0

--- a/solution.py
+++ b/solution.py
@@ -256,28 +256,45 @@
             jnp.bfloat16
         )
 
-    held = {(way, 0): frozen_weight.T for way in ("own", "up", "down")}
-
-    def send_z(hops, *before):
-        held["up", hops] = lax.ppermute(
-            tied(held["up", hops - 1], *before),
+    quarter = half // 2
+    held = {("whole", way, 0): frozen_weight.T for way in ("own", "up", "down")}
+
+    def send_z(name, hops, *before):
+        held[name, "up", hops] = lax.ppermute(
+            tied(held[name, "up", hops - 1], *before),
             "fsdp",
             [(i, i + 4) for i in range(fsdp_count - 4) if i // 4 >= hops - 1],
         )
-        held["down", hops] = lax.ppermute(
-            tied(held["down", hops - 1], *before),
+        held[name, "down", hops] = lax.ppermute(
+            tied(held[name, "down", hops - 1], *before),
             "fsdp",
             [(i, i - 4) for i in range(4, fsdp_count) if i // 4 + hops - 1 < depth],
         )
-        return held["up", hops], held["down", hops]
+        return held[name, "up", hops], held[name, "down", hops]
+
+    def by_z(position, wanted):
+        sources = [arrivals(plane, depth)[position] for plane in range(depth)]
+        arrays, keys, cases = [], [], []
+        for source in sources:
+            copies = []
+            for name, part, place in wanted:
+                key = (name, *source)
+                if name in lanes and source[1] <= 1:
+                    key = ("whole", *source)
+                    part = (all_lanes, lanes[name])
+                if key not in keys:
+                    keys.append(key)
+                    arrays.append(held[key])
+                copies.append((keys.index(key), part, place))
+            cases.append(copies)
+        return cases, arrays
 
     def own_block_at(position):
-        if position == 0:
-            return held["own", 0]
-        wanted = [arrivals(plane, depth)[position] for plane in range(depth)]
-        sources = sorted(set(wanted))
-        cases = [[(sources.index(w), all_lanes, all_lanes)] for w in wanted]
-        return assemble(z, cases, [held[w] for w in sources], (own_columns, in_rows))
+        wanted = [(name, all_lanes, (all_lanes, lanes[name])) for name in "cd"]
+        if not position:
+            return held["whole", "own", 0]
+        cases, arrays = by_z(position, wanted)
+        return assemble(z, cases, arrays, (own_columns, in_rows))
 
     finished = []
     running = None
@@ -291,10 +308,10 @@
         ]
 
     class Columns:
-        def __init__(self, copies, sources, slots):
+        def __init__(self, cases, sources, slots):
             self.slots = slots
             shape = (len(slots) * own_columns, in_rows)
-            self.weight = assemble(here, [copies], sources, shape)
+            self.weight = assemble(z, cases, sources, shape)
             finished.append(self)
 
         def of(self, matrix):
@@ -327,74 +344,104 @@
             running = tied(running + nn(self.of(gradient_slots), weight))
             return (running,)
 
+    def rows_of(number):
+        return slice(number * own_columns, (number + 1) * own_columns)
+
     def near(position):
         sources = [own[position], over_x[position], over_y[position]]
-        copies = [
-            (i, all_lanes, (slice(i * own_columns, (i + 1) * own_columns), all_lanes))
-            for i in range(3)
-        ]
-        return Columns(copies, sources, [4 * position + i for i in range(3)])
+        copies = [(i, all_lanes, (rows_of(i), all_lanes)) for i in range(3)]
+        return Columns([copies] * depth, sources, [4 * position + i for i in range(3)])
 
     def far(which):
-        copies, sources, slots = [], [], []
+        cases, sources, slots = [[] for _ in range(depth)], [], []
         for number, position in enumerate(which):
-            for name, (got, part) in zip("cd", ends[position]):
-                copies.append(
-                    (
-                        len(sources),
-                        slice(part * own_columns, (part + 1) * own_columns),
-                        (slice(number * own_columns, (number + 1) * own_columns), lanes[name]),
-                    )
-                )
+            rows = rows_of(number)
+            slots.append(4 * position + 3)
+            if position:
+                wanted = []
+                for i, name in enumerate("cd"):
+                    low = lanes[name].start
+                    part = (all_lanes, slice(i * quarter, (i + 1) * quarter))
+                    wanted.append(("far", part, (rows, slice(low, low + quarter))))
+                more, arrays = by_z(position, wanted)
+                for case, copies in zip(cases, more):
+                    case += [(len(sources) + i, part, place) for i, part, place in copies]
+                sources += arrays
+            for name, (got, index) in zip("cd", ends[position]):
+                low, high = lanes[name].start, lanes[name].stop
+                place = (rows, slice(low + quarter if position else low, high))
+                for case in cases:
+                    case.append((len(sources), rows_of(index), place))
                 sources.append(got)
-            slots.append(4 * position + 3)
-        return Columns(copies, sources, slots)
-
-    def start_far(which, *before):
-        halves = []
+        return Columns(cases, sources, slots)
+
+    def far_halves(which):
+        made = []
         for name, came in (("d", over_y), ("c", over_x)):
-            sources = [came[position] for position in which]
-            copies = [
-                (i, (all_lanes, lanes[name]), slice(i * own_columns, (i + 1) * own_columns))
-                for i in range(len(which))
-            ]
-            shape = (len(which) * own_columns, half)
-            halves.append(tied(assemble(here, [copies], sources, shape), *before))
-        got_d = lax.ppermute(halves[0], "fsdp", across_x)
-        got_c = lax.ppermute(halves[1], "fsdp", across_y)
+            low, high = lanes[name].start, lanes[name].stop
+            if which != [0]:
+                low += quarter
+            made.append(jnp.concatenate([came[position][:, low:high] for position in which]))
+        return made
+
+    def start_far(which, halves, *before):
+        got_d = lax.ppermute(tied(halves[0], *before), "fsdp", across_x)
+        got_c = lax.ppermute(tied(halves[1], *before), "fsdp", across_y)
         for number, position in enumerate(which):
             ends[position] = ((got_c, number), (got_d, number))
         return got_c, got_d
 
-    turns = [("near", [position]) for position in range(depth)]
-    turns += [("far", list(range(depth - 2))), ("far", [depth - 2]), ("far", [depth - 1])]
-    norms_turn = depth - 1
+    turns = [([0], [], 1), ([], [0], 1)]
+    turns += [([position], [], 2) for position in range(1, depth - 1)]
+    turns += [([depth - 1], list(range(1, depth - 1)), 3 * depth), ([], [depth - 1], 0)]
+    along_z = [("whole", 1)] + [(name, hops) for hops in range(2, depth) for name in "cd"]
+    along_z += [("far", hops) for hops in range(1, depth)]
+    norms_turn = 2
+    summed = False
+    sums_turn = depth
     own, over_x, over_y, ends = {}, {}, {}, {}
     squares = square_own
     token = work = ()
     arrived = []
     waiting = []
-    for number, (kind, which) in enumerate(turns):
+    for number, (near_planes, far_planes, count_z) in enumerate(turns):
         before = (token, work)
         token = ()
         work = ()
-        if kind == "near":
-            position = which[0]
+        for position in near_planes:
             own[position] = block = tied(own_block_at(position), *before)
             over_x[position] = lax.ppermute(block, "fsdp", across_x)
             over_y[position] = lax.ppermute(block, "fsdp", across_y)
             token += (over_x[position], over_y[position])
-            if position + 1 < depth:
-                token += send_z(position + 1, *before)
-        else:
-            token += start_far(which, *before)
+        if far_planes:
+            halves = far_halves(far_planes)
+            first = token
+            token += start_far(far_planes, halves, *before, first)
+        if number == norms_turn:
+            for bit in z_bits:
+                squares = widen(squares, bit, *before)
+        sent_z = squares if number == norms_turn else ()
+        for name, hops in along_z[:count_z]:
+            if name in lanes and hops == 2:
+                for way in ("up", "down"):
+                    held[name, way, 1] = held["whole", way, 1][:, lanes[name]]
+            if name == "far" and hops == 1:
+                (got_c, _), (got_d, _) = ends[0]
+                block = jnp.concatenate([got_c[:, :quarter], got_d[:, :quarter]], axis=1)
+                for way in ("own", "up", "down"):
+                    held["far", way, 0] = block
+            sent_z = send_z(name, hops, *before, sent_z)
+            token += sent_z
+            if number == sums_turn and not summed:
+                for bit in z_bits:
+                    sums = halve(sums, bit, before, sent_z)
+                summed = True
+                sent_z = (sums,)
+        along_z = along_z[count_z:]
 
         if number < 2:
             squares = widen(squares, (1, 2)[number], *before)
             work += (squares,)
-        if number == norms_turn:
-            for bit in z_bits:
-                squares = widen(squares, bit, *before)
         if number == norms_turn:
             col_norms = jnp.sqrt(squares + eps_norm)
             col_scale = magnitude / col_norms
@@ -408,26 +455,30 @@
             )
             running = nn(lowrank_gradient, down_t)
             work += (sums, running)
-        if number == norms_turn + 1:
-            for bit in z_bits:
-                sums = halve(sums, bit, before)
+        if number == sums_turn:
             sums = add(sums, 1)
             work += (sums,)
-        if number == norms_turn + 2:
+        if number == sums_turn + 1:
             sums = add(sums, 2, before)
-            work += (sums,)
-        if number == norms_turn + 3:
-            for bit in reversed(z_bits):
-                sums = widen(sums, bit, before)
 
         for columns in arrived:
             work += columns.forward(before)
             waiting.append(columns)
-        arrived = [near(which[0]) if kind == "near" else far(which)]
-        if number > norms_turn:
-            for columns in waiting[: 1 + (number == len(turns) - 1)]:
-                work += columns.backward(before) + columns.complete()
-            waiting = waiting[1 + (number == len(turns) - 1) :]
+        arrived = [near(position) for position in near_planes]
+        if number == sums_turn:
+            last_near = arrived.pop()
+            work += last_near.forward()
+        if far_planes:
+            arrived.append(far(far_planes))
+        if number == sums_turn:
+            for columns in waiting:
+                work += columns.complete()
+                if len(columns.slots) == 3:
+                    work += columns.backward(before)
+            done = waiting
+            waiting = [last_near]
+    for bit in reversed(z_bits):
+        sums = widen(sums, bit)
     in_sum = sums[:, :in_rows].astype(jnp.float32)
     up_sum = sums[:, in_rows:].astype(jnp.float32)
 
@@ -436,6 +487,7 @@
         waiting.append(columns)
     for columns in waiting:
         columns.complete()
+    waiting = [columns for columns in done if len(columns.slots) != 3] + waiting
     input_gradient = last_gradient(
         [columns.of(gradient_slots) for columns in waiting],
         [columns.weight for columns in waiting],

time: 419 us -> 411 us (0.981)
  waiting for transfers between devices: 157 us -> 126 us
  starting transfers between devices: 46.8 us -> 68.3 us
  local copies, waits for them, and re-layouts: 28 us -> 47.6 us
  Pallas kernels: 55.3 us -> 43.8 us
  matrix products: 94.1 us -> 88.8 us
    ppermute x17, waiting for transfers between devices: 101 us -> 56 us  [flip(): return lax.ppermute(value, axis, pairs)]
    ppermute x12 -> x22, waiting for transfers between devices: 49.9 us -> 69.5 us  [the longest x8 56.9 us: send_z(): lax.ppermute(tied(held[name, 'down', hops - 1], *before), 'fsdp', [(i, i...]
    ppermute x12 -> x22, starting transfers between devices: 21.1 us -> 38 us  [the longest x8 19.6 us: send_z(): lax.ppermute(tied(held[name, 'up', hops - 1], *before), 'fsdp', [(i, i +...]
    pallas_call x16 -> x10, Pallas kernels: 31 us -> 15.9 us  [assemble(): pl.pallas_call(functools.partial(assemble_kernel, cases), in_specs=[pl.Bl...]
    slice x0 -> x14, local copies, waits for them, and re-layouts: none -> 12.9 us  [the longest x10 8.6 us: far_halves(): came[position][:, low:high]]
    dot_general x14 -> x13, matrix products: 51.1 us -> 41.3 us  [nn(): return jnp.dot(a, b, preferred_element_type=jnp.float32)]
    ppermute x17, starting transfers between devices: 15.6 us -> 21.4 us  [flip(): return lax.ppermute(value, axis, pairs)]
    ppermute x4, waiting for transfers between devices: 4.79 us -> 0.01 us  [on_device(): over_y[position] = lax.ppermute(block, 'fsdp', across_y)]
  transfers between devices with their start and end apart: 46 -> 56, of which waited for: 14 -> 20; matrix products, arithmetic and copies ran while one was open for 29% -> 32% of each run, Pallas kernels for 11% -> 10%
where the time goes in v1:
time: 411 us; the launch traced here: 403 us
  waiting for transfers between devices  126 us (31%)
  matrix products  88.8 us (22%)
  starting transfers between devices  68.3 us (17%)
  local copies, waits for them, and re-layouts  47.6 us (12%)
  Pallas kernels  43.8 us (11%)
  between operations  16.1 us (4%)
  other arithmetic  12.7 us (3%)
    ppermute x8, waiting for transfers between devices, send_z(): lax.ppermute(tied(held[name, 'down', hops - 1], *before), 'fsdp', [(i, i...  56.9 us
    ppermute x17, waiting for transfers between devices, flip(): return lax.ppermute(value, axis, pairs)  56 us
    dot_general x16, matrix products, nt(): lax.dot_general(a, b, (((1,), (1,)), ((), ())), preferred_element_type=jn...  42.3 us
    dot_general x13, matrix products, nn(): return jnp.dot(a, b, preferred_element_type=jnp.float32)  41.3 us
    unnamed x179, local copies, waits for them, and re-layouts  24.1 us
    ppermute x17, starting transfers between devices, flip(): return lax.ppermute(value, axis, pairs)  21.4 us
    ppermute x8, starting transfers between devices, send_z(): lax.ppermute(tied(held[name, 'up', hops - 1], *before), 'fsdp', [(i, i +...  19.6 us
    pallas_call x10, Pallas kernels, assemble(): pl.pallas_call(functools.partial(assemble_kernel, cases), in_specs=[pl.Bl...  15.9 us
  transfers between devices with their start and end apart: 56, of which 20 were waited for; matrix products, arithmetic and copies ran while one was open for 32% of the time, Pallas kernels for 10%

profile of v1, /device:TPU:0, one launch (start us, length us, event | category | flops | bytes accessed | tf_op | source)
XLA Modules:
  0.0 402.8 jit_solution(793796375771753326)
XLA Ops:
  7.2 4.1 %copy.31 = bf16[4096,256]{0,1:T(8,128)(2,1)} copy(bf16[4096,256]{1,0:T(8,128)(2,1)} %param.16) | data formatting | bytes 4194304 | tf_op args[1]
  12.8 7.0 %collective-permute-start.2 = (bf16[256,4096]{1,0:T(8,128)(2,1)}, bf16[256,4096]{1,0:T(8,128)(2,1)}, u32[]{:S(2)}, u32[]{:S(2)}) collective-permute-start(bf16[256,4096]{1,0:T(8,128)(2,1)} %bitcast.111), channel_id=1, source_target_pairs={{0,8},{2,10},{4,12},{6,14},{8,16},{10,18},{12,20},{14,22},{16,24},... | collective-permute-start | bytes 6291464 | tf_op jit(solution)/shard_map/ppermute | solution.py:263
  23.2 2.5 fusion.9
  30.2 4.7 %fusion.66 = f32[512,64]{1,0:T(8,128)} fusion(bf16[512,4096]{1,0:T(8,128)(2,1)} %param.15, bf16[4096,64]{0,1:T(8,128)(2,1)S(1)} %copy-done), kind=kOutput, calls=%fused_computation.166 | convolution fusion | flops 268435456 | bytes 4849664 | tf_op jit(solution)/shard_map/dot_general | solution.py:56
  37.7 30.9 %collective-permute-done.5 = f32[256]{0:T(256)S(1)} collective-permute-done((f32[256]{0:T(256)S(1)}, f32[256]{0:T(256)S(1)}, u32[]{:S(2)}, u32[]{:S(2)}) %collective-permute-start.5) | collective-permute-done | bytes 1056 | tf_op jit(solution)/shard_map/ppermute | solution.py:14
  69.9 2.1 fusion.23
  73.4 2.9 fusion.60
  83.3 2.5 shard_map.182
  87.3 3.4 fusion.10.refs_0_
  92.5 2.7 constant_dynamic-update-slice_fusion.18
  96.2 8.3 %collective-permute-done.9.refs_0_ = bf16[256,2048]{1,0:T(8,128)(2,1)S(1)} collective-permute-done((bf16[256,2048]{1,0:T(8,128)(2,1)S(1)}, bf16[256,2048]{1,0:T(8,128)(2,1)S(1)}, u32[]{:S(2)}, u32[]{:S(2)}) %collective-permute-start.9) | collective-permute-done | bytes 1048608 | tf_op jit(solution)/shard_map/ppermute | solution.py:389
  105.9 7.8 %collective-permute-done.12.refs_0_.refs_2_ = bf16[256,2048]{1,0:T(8,128)(2,1)S(1)} collective-permute-done((bf16[256,2048]{1,0:T(8,128)(2,1)S(1)}, bf16[256,2048]{1,0:T(8,128)(2,1)S(1)}, u32[]{:S(2)}, u32[]{:S(2)}) %collective-permute-start.12) | collective-permute-done | bytes 1048608 | tf_op jit(solution)/shard_map/ppermute | solution.py:268
  117.2 2.0 fusion.15.refs_0_
  121.8 3.5 collective-permute-done.14
  132.0 2.2 copy-done.12
  147.3 5.9 %collective-permute-done.19.refs_1_.refs_3_ = bf16[256,2048]{1,0:T(8,128)(2,1)} collective-permute-done((bf16[256,2048]{1,0:T(8,128)(2,1)}, bf16[256,2048]{1,0:T(8,128)(2,1)}, u32[]{:S(2)}, u32[]{:S(2)}) %collective-permute-start.19) | collective-permute-done | bytes 1048608 | tf_op jit(solution)/shard_map/ppermute | solution.py:268
  155.2 4.7 %fusion.68 = f32[512,4096]{1,0:T(8,128)} fusion(bf16[512,64]{0,1:T(8,128)(2,1)S(1)} %convolution_convert_fusion.7, bf16[4096,64]{0,1:T(8,128)(2,1)S(1)} %copy-done), kind=kOutput, calls=%fused_computation.168 | convolution fusion | flops 268435456 | bytes 8978432 | tf_op jit(solution)/shard_map/dot_general | solution.py:56
  162.1 17.2 %collective-permute-done.21.refs_0_ = bf16[256,2048]{1,0:T(8,128)(2,1)S(1)} collective-permute-done((bf16[256,2048]{1,0:T(8,128)(2,1)S(1)}, bf16[256,2048]{1,0:T(8,128)(2,1)S(1)}, u32[]{:S(2)}, u32[]{:S(2)}) %collective-permute-start.21) | collective-permute-done | bytes 1048608 | tf_op jit(solution)/shard_map/ppermute | solution.py:268
  184.5 3.0 shard_map.190
  188.5 3.5 fusion.11.refs_0_
  192.1 15.0 %collective-permute-done.26.refs_1_ = bf16[256,2048]{1,0:T(8,128)(2,1)S(1)} collective-permute-done((bf16[256,2048]{1,0:T(8,128)(2,1)}, bf16[256,2048]{1,0:T(8,128)(2,1)S(1)}, u32[]{:S(2)}, u32[]{:S(2)}) %collective-permute-start.26) | collective-permute-done | bytes 1048608 | tf_op jit(solution)/shard_map/ppermute | solution.py:268
  208.4 5.5 %collective-permute-start.27 = (bf16[256,2048]{1,0:T(8,128)(2,1)S(1)}, bf16[256,2048]{1,0:T(8,128)(2,1)}, u32[]{:S(2)}, u32[]{:S(2)}) collective-permute-start(bf16[256,2048]{1,0:T(8,128)(2,1)S(1)} %copy-done.63), channel_id=1, source_target_pairs={{0,8},{2,10},{4,12},{6,14},{8,16},{10,18},{12,20},{14,22},{16,24},... | collective-permute-start | bytes 3145736 | tf_op jit(solution)/shard_map/ppermute | solution.py:263
  213.9 2.0 fusion.56
  219.7 2.7 constant_dynamic-update-slice_fusion.16
  224.7 5.5 %collective-permute-done.28.refs_0_.refs_5_ = bf16[256,2048]{1,0:T(8,128)(2,1)} collective-permute-done((bf16[256,2048]{1,0:T(8,128)(2,1)S(1)}, bf16[256,2048]{1,0:T(8,128)(2,1)}, u32[]{:S(2)}, u32[]{:S(2)}) %collective-permute-start.28) | collective-permute-done | bytes 1048608 | tf_op jit(solution)/shard_map/ppermute | solution.py:268
  235.1 8.4 %convolution_add_fusion.2 = f32[512,4096]{1,0:T(8,128)} fusion(f32[512,4096]{1,0:T(8,128)} %fusion.68, bf16[768,4096]{1,0:T(8,128)(2,1)S(1)} %bitcast.107, bf16[512,4096]{1,0:T(8,128)(2,1)} %copy-done.47), kind=kOutput, calls=%fused_computation.5 | convolution fusion | flops 3223322624 | bytes 23855104 | tf_op jit(solution)/shard_map/dot_general | solution.py:56
  247.4 4.4 %fusion.12.refs_0_ = bf16[512,768]{1,0:T(8,128)(2,1)} fusion(bf16[768,4096]{1,0:T(8,128)(2,1)S(1)} %shard_map.193, bf16[512,4096]{1,0:T(8,128)(2,1)S(1)} %copy-done.56), kind=kOutput, calls=%fused_computation.28 | convolution fusion | flops 3221618688 | bytes 11272192 | tf_op jit(solution)/shard_map/dot_general | solution.py:52
  251.8 6.9 %convolution_add_fusion.1 = f32[512,4096]{1,0:T(8,128)} fusion(f32[512,4096]{1,0:T(8,128)S(1)} %bitcast.120, bf16[768,4096]{1,0:T(8,128)(2,1)S(1)} %shard_map.190, bf16[512,4096]{1,0:T(8,128)(2,1)} %copy-done.47), kind=kOutput, calls=%fused_computation.4 | convolution fusion | flops 3223322624 | bytes 23855104 | tf_op jit(solution)/shard_map/dot_general | solution.py:56
  258.8 6.2 %convolution_add_fusion.refs_8_ = f32[512,4096]{1,0:T(8,128)S(1)} fusion(f32[512,4096]{1,0:T(8,128)} %convolution_add_fusion.1, bf16[768,4096]{1,0:T(8,128)(2,1)S(1)} %shard_map.193, bf16[512,4096]{1,0:T(8,128)(2,1)} %copy-done.47), kind=kOutput, calls=%fused_computation.3 | convolution fusion | flops 3223322624 | bytes 23855104 | tf_op jit(solution)/shard_map/dot_general | solution.py:56
  266.1 5.5 %collective-permute-start.37 = (bf16[64,3072]{1,0:T(8,128)(2,1)}, bf16[64,3072]{1,0:T(8,128)(2,1)S(1)}, u32[]{:S(2)}, u32[]{:S(2)}) collective-permute-start(bf16[64,3072]{1,0:T(8,128)(2,1)} %select_convert_fusion), channel_id=1, source_target_pairs={{0,8},{2,10},{4,12},{6,14},{8,0},{10,2},{12,4},{14,6},{16,24},{18,... | collective-permute-start | bytes 1179656 | tf_op jit(solution)/shard_map/ppermute | solution.py:14
  271.6 2.7 constant_dynamic-update-slice_fusion.15
  276.5 2.8 shard_map.194
  279.3 2.3 collective-permute-done.37
  283.0 10.6 %collective-permute-done.38 = bf16[64,1536]{1,0:T(8,128)(2,1)S(1)} collective-permute-done((bf16[64,1536]{1,0:T(8,128)(2,1)S(1)}, bf16[64,1536]{1,0:T(8,128)(2,1)S(1)}, u32[]{:S(2)}, u32[]{:S(2)}) %collective-permute-start.38) | collective-permute-done | bytes 196640 | tf_op jit(solution)/shard_map/ppermute | solution.py:14
  300.2 2.6 shard_map.196.refs_5_
  302.8 7.9 %fusion.13.refs_0_ = bf16[512,768]{1,0:T(8,128)(2,1)S(1)} fusion(bf16[768,4096]{1,0:T(8,128)(2,1)S(1)} %shard_map.196.refs_5_, bf16[512,4096]{1,0:T(8,128)(2,1)} %param.15), kind=kOutput, calls=%fused_computation.29 | convolution fusion | flops 3221618688 | bytes 11272192 | tf_op jit(solution)/shard_map/dot_general | solution.py:52
  313.2 2.8 constant_dynamic-update-slice_fusion.14
  318.0 4.5 %collective-permute-done.40.refs_0_ = bf16[256,2048]{1,0:T(8,128)(2,1)} collective-permute-done((bf16[256,2048]{1,0:T(8,128)(2,1)S(1)}, bf16[256,2048]{1,0:T(8,128)(2,1)}, u32[]{:S(2)}, u32[]{:S(2)}) %collective-permute-start.40) | collective-permute-done | bytes 1048608 | tf_op jit(solution)/shard_map/ppermute | solution.py:268
  328.1 2.4 fusion.14.refs_0_
  333.8 3.7 collective-permute-start.47
  337.6 2.1 fusion.17
  339.7 2.0 collective-permute-done.47
  347.3 2.5 collective-permute-start.48
  357.3 2.8 copy-done.2
  360.1 11.5 %shard_map.203 = bf16[512,4096]{1,0:T(8,128)(2,1)} custom-call(bf16[512,256]{1,0:T(8,128)(2,1)S(1)} %copy-done.31, bf16[512,768]{1,0:T(8,128)(2,1)S(1)} %copy-done.29, bf16[512,512]{1,0:T(8,128)(2,1)S(1)} %pad_maximum_fusion.6.refs_2_, bf16[512,256]{1,0:T(8,128)(2,1)S(1)} %get-tuple-element.107.refs_3_, bf16[256,4096]{1,0:T(8,128)(2,1)S(1)} %shard_map.187.refs_4_, ...), custom_call_target="tpu_custom_call" | custom-call | tf_op jit(solution)/shard_map/pallas_call | solution.py:116
  373.0 2.4 collective-permute-done.51
  377.9 4.1 %shard_map.202 = bf16[512,2048]{1,0:T(8,128)(2,1)} custom-call(s32[8]{0:T(128)S(1)} %copy-done.43, bf16[512,4096]{1,0:T(8,128)(2,1)} %constant_dynamic-update-slice_fusion.source), custom_call_target="tpu_custom_call" | custom-call | tf_op jit(solution)/shard_map/pallas_call | solution.py:168
  389.9 2.6 multiply_bitcast_fusion
  (382 shorter events, 131.5 us)
Async XLA Ops:
  7.2 124.8 %all-gather.2.cloned.1.call-start = ((), (), s32[]{:S(2)}) async-start(), calls=%async_computation | async-start | bytes 6291456 | tf_op jit(solution)/shard_map/all_gather | solution.py:226
  11.4 60.7 %collective-permute-start.3 = (bf16[256,4096]{1,0:T(8,128)(2,1)}, bf16[256,4096]{1,0:T(8,128)(2,1)S(1)}, u32[]{:S(2)}, u32[]{:S(2)}) collective-permute-start(bf16[256,4096]{1,0:T(8,128)(2,1)} %bitcast.110), channel_id=1, source_target_pairs={{8,0},{10,2},{12,4},{14,6},{16,8},{18,10},{20,12},{22,14},{24,16},... | collective-permute-start | bytes 6291464 | tf_op jit(solution)/shard_map/ppermute | solution.py:268
  12.8 60.6 %collective-permute-start.2 = (bf16[256,4096]{1,0:T(8,128)(2,1)}, bf16[256,4096]{1,0:T(8,128)(2,1)}, u32[]{:S(2)}, u32[]{:S(2)}) collective-permute-start(bf16[256,4096]{1,0:T(8,128)(2,1)} %bitcast.111), channel_id=1, source_target_pairs={{0,8},{2,10},{4,12},{6,14},{8,16},{10,18},{12,20},{14,22},{16,24},... | collective-permute-start | bytes 6291464 | tf_op jit(solution)/shard_map/ppermute | solution.py:263
  19.8 56.6 %collective-permute-start.1 = (bf16[256,4096]{1,0:T(8,128)(2,1)}, bf16[256,4096]{1,0:T(8,128)(2,1)}, u32[]{:S(2)}, u32[]{:S(2)}) collective-permute-start(bf16[256,4096]{1,0:T(8,128)(2,1)} %bitcast.112), channel_id=1, source_target_pairs={{0,4},{2,6},{4,0},{6,2},{8,12},{10,14},{12,8},{14,10},{16,20},{18,... | collective-permute-start | bytes 6291464 | tf_op jit(solution)/shard_map/ppermute | solution.py:414
  21.7 54.6 %collective-permute-start = (bf16[256,4096]{1,0:T(8,128)(2,1)}, bf16[256,4096]{1,0:T(8,128)(2,1)}, u32[]{:S(2)}, u32[]{:S(2)}) collective-permute-start(bf16[256,4096]{1,0:T(8,128)(2,1)} %bitcast.113), channel_id=1, source_target_pairs={{0,2},{2,0},{4,6},{6,4},{8,10},{10,8},{12,14},{14,12},{16,18},{18,... | collective-permute-start | bytes 6291464 | tf_op jit(solution)/shard_map/ppermute | solution.py:413
  25.7 9.3 %collective-permute-start.4 = (f32[256]{0:T(256)S(1)}, f32[256]{0:T(256)S(1)}, u32[]{:S(2)}, u32[]{:S(2)}) collective-permute-start(f32[256]{0:T(256)S(1)} %fusion.9), channel_id=1, source_target_pairs={{0,1},{1,0},{2,3},{3,2},{4,5},{5,4},{6,7},{7,6},{8,9},{9,8},{10,11... | collective-permute-start | bytes 3080 | tf_op jit(solution)/shard_map/ppermute | solution.py:14
  35.0 33.6 %collective-permute-start.5 = (f32[256]{0:T(256)S(1)}, f32[256]{0:T(256)S(1)}, u32[]{:S(2)}, u32[]{:S(2)}) collective-permute-start(f32[256]{0:T(256)S(1)} %add.237), channel_id=1, source_target_pairs={{0,2},{2,0},{4,6},{6,4},{8,10},{10,8},{12,14},{14,12},{16,18},{18,... | collective-permute-start | bytes 3080 | tf_op jit(solution)/shard_map/ppermute | solution.py:14
  69.8 16.1 %collective-permute-start.7 = (f32[512,64]{1,0:T(8,128)}, f32[512,64]{1,0:T(8,128)S(1)}, u32[]{:S(2)}, u32[]{:S(2)}) collective-permute-start(f32[512,64]{1,0:T(8,128)} %fusion.66), channel_id=1, source_target_pairs={{0,1},{1,0},{2,3},{3,2},{4,5},{5,4},{6,7},{7,6},{8,9},{9,8},{10,11... | collective-permute-start | bytes 393224 | tf_op jit(solution)/shard_map/ppermute | solution.py:14
  77.6 13.2 %collective-permute-start.8 = (f32[512]{0:T(512)S(1)}, f32[512]{0:T(512)S(1)}, u32[]{:S(2)}, u32[]{:S(2)}) collective-permute-start(f32[512]{0:T(512)S(1)} %pad_maximum_fusion.12), channel_id=1, source_target_pairs={{0,4},{2,6},{4,0},{6,2},{8,12},{10,14},{12,8},{14,10},{16,20},{18,... | collective-permute-start | bytes 6152 | tf_op jit(solution)/shard_map/ppermute | solution.py:14
  79.3 25.2 %collective-permute-start.9 = (bf16[256,2048]{1,0:T(8,128)(2,1)S(1)}, bf16[256,2048]{1,0:T(8,128)(2,1)S(1)}, u32[]{:S(2)}, u32[]{:S(2)}) collective-permute-start(bf16[256,2048]{1,0:T(8,128)(2,1)S(1)} %slice.316), channel_id=1, source_target_pairs={{0,4},{2,6},{4,0},{6,2},{8,12},{10,14},{12,8},{14,10},{16,20},{18,... | collective-permute-start | bytes 3145736 | tf_op jit(solution)/shard_map/ppermute | solution.py:389
  81.1 24.8 %collective-permute-start.10 = (bf16[256,2048]{1,0:T(8,128)(2,1)S(1)}, bf16[256,2048]{1,0:T(8,128)(2,1)S(1)}, u32[]{:S(2)}, u32[]{:S(2)}) collective-permute-start(bf16[256,2048]{1,0:T(8,128)(2,1)S(1)} %slice.317), channel_id=1, source_target_pairs={{0,2},{2,0},{4,6},{6,4},{8,10},{10,8},{12,14},{14,12},{16,18},{18,... | collective-permute-start | bytes 3145736 | tf_op jit(solution)/shard_map/ppermute | solution.py:388
  82.6 23.4 %collective-permute-start.11 = (bf16[256,2048]{1,0:T(8,128)(2,1)S(1)}, bf16[256,2048]{1,0:T(8,128)(2,1)S(1)}, u32[]{:S(2)}, u32[]{:S(2)}) collective-permute-start(bf16[256,2048]{1,0:T(8,128)(2,1)S(1)} %get-tuple-element.59), channel_id=1, source_target_pairs={{8,16},{10,18},{12,20},{14,22},{16,24},{18,26},{20,28},{22,30},{9,... | collective-permute-start | bytes 3145736 | tf_op jit(solution)/shard_map/ppermute | solution.py:263
  85.9 27.8 %collective-permute-start.12 = (bf16[256,2048]{1,0:T(8,128)(2,1)S(1)}, bf16[256,2048]{1,0:T(8,128)(2,1)S(1)}, u32[]{:S(2)}, u32[]{:S(2)}) collective-permute-start(bf16[256,2048]{1,0:T(8,128)(2,1)S(1)} %get-tuple-element.60), channel_id=1, source_target_pairs={{8,0},{10,2},{12,4},{14,6},{16,8},{18,10},{20,12},{22,14},{9,1},{1... | collective-permute-start | bytes 3145736 | tf_op jit(solution)/shard_map/ppermute | solution.py:268
  113.7 48.4 %collective-permute-start.17 = (bf16[256,4096]{1,0:T(8,128)(2,1)}, bf16[256,4096]{1,0:T(8,128)(2,1)}, u32[]{:S(2)}, u32[]{:S(2)}) collective-permute-start(bf16[256,4096]{1,0:T(8,128)(2,1)} %shard_map.189.refs_0_), channel_id=1, source_target_pairs={{0,4},{2,6},{4,0},{6,2},{8,12},{10,14},{12,8},{14,10},{16,20},{18,... | collective-permute-start | bytes 6291464 | tf_op jit(solution)/shard_map/ppermute | solution.py:414
  114.2 47.9 %collective-permute-start.16 = (bf16[256,4096]{1,0:T(8,128)(2,1)}, bf16[256,4096]{1,0:T(8,128)(2,1)}, u32[]{:S(2)}, u32[]{:S(2)}) collective-permute-start(bf16[256,4096]{1,0:T(8,128)(2,1)} %shard_map.189.refs_0_), channel_id=1, source_target_pairs={{0,2},{2,0},{4,6},{6,4},{8,10},{10,8},{12,14},{14,12},{16,18},{18,... | collective-permute-start | bytes 6291464 | tf_op jit(solution)/shard_map/ppermute | solution.py:413
  120.6 23.6 %collective-permute-start.15 = (bf16[512,256]{1,0:T(8,128)(2,1)}, bf16[512,256]{1,0:T(8,128)(2,1)}, u32[]{:S(2)}, u32[]{:S(2)}) collective-permute-start(bf16[512,256]{1,0:T(8,128)(2,1)} %fusion.15.refs_0_), channel_id=1, source_target_pairs={{0,1},{1,0},{2,3},{3,2},{4,5},{5,4},{6,7},{7,6},{8,9},{9,8},{10,11... | collective-permute-start | bytes 786440 | tf_op jit(solution)/shard_map/ppermute | solution.py:304
  126.5 26.6 %collective-permute-start.19 = (bf16[256,2048]{1,0:T(8,128)(2,1)}, bf16[256,2048]{1,0:T(8,128)(2,1)}, u32[]{:S(2)}, u32[]{:S(2)}) collective-permute-start(bf16[256,2048]{1,0:T(8,128)(2,1)} %get-tuple-element.68), channel_id=1, source_target_pairs={{8,0},{10,2},{12,4},{14,6},{16,8},{18,10},{20,12},{22,14},{9,1},{1... | collective-permute-start | bytes 3145736 | tf_op jit(solution)/shard_map/ppermute | solution.py:268
  127.8 25.3 %collective-permute-start.18 = (bf16[256,2048]{1,0:T(8,128)(2,1)}, bf16[256,2048]{1,0:T(8,128)(2,1)}, u32[]{:S(2)}, u32[]{:S(2)}) collective-permute-start(bf16[256,2048]{1,0:T(8,128)(2,1)} %get-tuple-element.67), channel_id=1, source_target_pairs={{8,16},{10,18},{12,20},{14,22},{16,24},{18,26},{20,28},{22,30},{9,... | collective-permute-start | bytes 3145736 | tf_op jit(solution)/shard_map/ppermute | solution.py:263
  153.1 8.9 %collective-permute-start.20 = (bf16[256,2048]{1,0:T(8,128)(2,1)S(1)}, bf16[256,2048]{1,0:T(8,128)(2,1)S(1)}, u32[]{:S(2)}, u32[]{:S(2)}) collective-permute-start(bf16[256,2048]{1,0:T(8,128)(2,1)S(1)} %copy-done.14), channel_id=1, source_target_pairs={{16,24},{18,26},{20,28},{22,30},{17,25},{19,27},{21,29},{23,31}} | collective-permute-start | bytes 3145736 | tf_op jit(solution)/shard_map/ppermute | solution.py:263
  153.9 25.4 %collective-permute-start.21 = (bf16[256,2048]{1,0:T(8,128)(2,1)S(1)}, bf16[256,2048]{1,0:T(8,128)(2,1)S(1)}, u32[]{:S(2)}, u32[]{:S(2)}) collective-permute-start(bf16[256,2048]{1,0:T(8,128)(2,1)S(1)} %copy-done.16), channel_id=1, source_target_pairs={{8,0},{10,2},{12,4},{14,6},{9,1},{11,3},{13,5},{15,7}} | collective-permute-start | bytes 3145736 | tf_op jit(solution)/shard_map/ppermute | solution.py:268
  179.3 52.0 %collective-permute-start.24 = (bf16[256,4096]{1,0:T(8,128)(2,1)S(1)}, bf16[256,4096]{1,0:T(8,128)(2,1)S(1)}, u32[]{:S(2)}, u32[]{:S(2)}) collective-permute-start(bf16[256,4096]{1,0:T(8,128)(2,1)S(1)} %shard_map.192.refs_0_), channel_id=1, source_target_pairs={{0,4},{2,6},{4,0},{6,2},{8,12},{10,14},{12,8},{14,10},{16,20},{18,... | collective-permute-start | bytes 6291464 | tf_op jit(solution)/shard_map/ppermute | solution.py:414
  180.8 51.9 %collective-permute-start.23 = (bf16[256,4096]{1,0:T(8,128)(2,1)S(1)}, bf16[256,4096]{1,0:T(8,128)(2,1)S(1)}, u32[]{:S(2)}, u32[]{:S(2)}) collective-permute-start(bf16[256,4096]{1,0:T(8,128)(2,1)S(1)} %shard_map.192.refs_0_), channel_id=1, source_target_pairs={{0,2},{2,0},{4,6},{6,4},{8,10},{10,8},{12,14},{14,12},{16,18},{18,... | collective-permute-start | bytes 6291464 | tf_op jit(solution)/shard_map/ppermute | solution.py:413
  182.3 9.8 %collective-permute-start.25 = (bf16[256,2048]{1,0:T(8,128)(2,1)}, bf16[256,2048]{1,0:T(8,128)(2,1)S(1)}, u32[]{:S(2)}, u32[]{:S(2)}) collective-permute-start(bf16[256,2048]{1,0:T(8,128)(2,1)} %collective-permute-done.18.refs_4_.refs_5_), channel_id=1, source_target_pairs={{16,24},{18,26},{20,28},{22,30},{17,25},{19,27},{21,29},{23,31}} | collective-permute-start | bytes 3145736 | tf_op jit(solution)/shard_map/ppermute | solution.py:263
  183.0 24.1 %collective-permute-start.26 = (bf16[256,2048]{1,0:T(8,128)(2,1)}, bf16[256,2048]{1,0:T(8,128)(2,1)S(1)}, u32[]{:S(2)}, u32[]{:S(2)}) collective-permute-start(bf16[256,2048]{1,0:T(8,128)(2,1)} %collective-permute-done.19.refs_1_.refs_3_), channel_id=1, source_target_pairs={{8,0},{10,2},{12,4},{14,6},{9,1},{11,3},{13,5},{15,7}} | collective-permute-start | bytes 3145736 | tf_op jit(solution)/shard_map/ppermute | solution.py:268
  192.0 30.4 %collective-permute-start.22 = (bf16[512,768]{1,0:T(8,128)(2,1)S(1)}, bf16[512,768]{1,0:T(8,128)(2,1)S(1)}, u32[]{:S(2)}, u32[]{:S(2)}) collective-permute-start(bf16[512,768]{1,0:T(8,128)(2,1)S(1)} %fusion.11.refs_0_), channel_id=1, source_target_pairs={{0,1},{1,0},{2,3},{3,2},{4,5},{5,4},{6,7},{7,6},{8,9},{9,8},{10,11... | collective-permute-start | bytes 2359304 | tf_op jit(solution)/shard_map/ppermute | solution.py:304
  207.1 23.1 %collective-permute-start.28 = (bf16[256,2048]{1,0:T(8,128)(2,1)S(1)}, bf16[256,2048]{1,0:T(8,128)(2,1)}, u32[]{:S(2)}, u32[]{:S(2)}) collective-permute-start(bf16[256,2048]{1,0:T(8,128)(2,1)S(1)} %copy-done.63), channel_id=1, source_target_pairs={{8,0},{10,2},{12,4},{14,6},{16,8},{18,10},{20,12},{22,14},{24,16},... | collective-permute-start | bytes 3145736 | tf_op jit(solution)/shard_map/ppermute | solution.py:268
  208.4 22.9 %collective-permute-start.27 = (bf16[256,2048]{1,0:T(8,128)(2,1)S(1)}, bf16[256,2048]{1,0:T(8,128)(2,1)}, u32[]{:S(2)}, u32[]{:S(2)}) collective-permute-start(bf16[256,2048]{1,0:T(8,128)(2,1)S(1)} %copy-done.63), channel_id=1, source_target_pairs={{0,8},{2,10},{4,12},{6,14},{8,16},{10,18},{12,20},{14,22},{16,24},... | collective-permute-start | bytes 3145736 | tf_op jit(solution)/shard_map/ppermute | solution.py:263
  234.0 64.0 %collective-permute-start.31 = (bf16[256,4096]{1,0:T(8,128)(2,1)S(1)}, bf16[256,4096]{1,0:T(8,128)(2,1)}, u32[]{:S(2)}, u32[]{:S(2)}) collective-permute-start(bf16[256,4096]{1,0:T(8,128)(2,1)S(1)} %shard_map.195.refs_0_), channel_id=1, source_target_pairs={{0,4},{2,6},{4,0},{6,2},{8,12},{10,14},{12,8},{14,10},{16,20},{18,... | collective-permute-start | bytes 6291464 | tf_op jit(solution)/shard_map/ppermute | solution.py:414
  234.5 63.5 %collective-permute-start.30 = (bf16[256,4096]{1,0:T(8,128)(2,1)S(1)}, bf16[256,4096]{1,0:T(8,128)(2,1)}, u32[]{:S(2)}, u32[]{:S(2)}) collective-permute-start(bf16[256,4096]{1,0:T(8,128)(2,1)S(1)} %shard_map.195.refs_0_), channel_id=1, source_target_pairs={{0,2},{2,0},{4,6},{6,4},{8,10},{10,8},{12,14},{14,12},{16,18},{18,... | collective-permute-start | bytes 6291464 | tf_op jit(solution)/shard_map/ppermute | solution.py:413
  243.5 22.6 %collective-permute-start.35 = (bf16[256,2048]{1,0:T(8,128)(2,1)}, bf16[256,2048]{1,0:T(8,128)(2,1)S(1)}, u32[]{:S(2)}, u32[]{:S(2)}) collective-permute-start(bf16[256,2048]{1,0:T(8,128)(2,1)} %collective-permute-done.28.refs_0_.refs_5_), channel_id=1, source_target_pairs={{8,0},{10,2},{12,4},{14,6},{16,8},{18,10},{20,12},{22,14},{9,1},{1... | collective-permute-start | bytes 3145736 | tf_op jit(solution)/shard_map/ppermute | solution.py:268
  245.0 21.1 %collective-permute-start.36 = (bf16[256,2048]{1,0:T(8,128)(2,1)}, bf16[256,2048]{1,0:T(8,128)(2,1)}, u32[]{:S(2)}, u32[]{:S(2)}) collective-permute-start(bf16[256,2048]{1,0:T(8,128)(2,1)} %collective-permute-done.27.refs_1_), channel_id=1, source_target_pairs={{8,16},{10,18},{12,20},{14,22},{16,24},{18,26},{20,28},{22,30},{9,... | collective-permute-start | bytes 3145736 | tf_op jit(solution)/shard_map/ppermute | solution.py:263
  251.8 24.6 %collective-permute-start.29 = (bf16[512,768]{1,0:T(8,128)(2,1)}, bf16[512,768]{1,0:T(8,128)(2,1)}, u32[]{:S(2)}, u32[]{:S(2)}) collective-permute-start(bf16[512,768]{1,0:T(8,128)(2,1)} %fusion.12.refs_0_), channel_id=1, source_target_pairs={{0,1},{1,0},{2,3},{3,2},{4,5},{5,4},{6,7},{7,6},{8,9},{9,8},{10,11... | collective-permute-start | bytes 2359304 | tf_op jit(solution)/shard_map/ppermute | solution.py:304
  266.1 15.5 %collective-permute-start.37 = (bf16[64,3072]{1,0:T(8,128)(2,1)}, bf16[64,3072]{1,0:T(8,128)(2,1)S(1)}, u32[]{:S(2)}, u32[]{:S(2)}) collective-permute-start(bf16[64,3072]{1,0:T(8,128)(2,1)} %select_convert_fusion), channel_id=1, source_target_pairs={{0,8},{2,10},{4,12},{6,14},{8,0},{10,2},{12,4},{14,6},{16,24},{18,... | collective-permute-start | bytes 1179656 | tf_op jit(solution)/shard_map/ppermute | solution.py:14
  281.7 11.9 %collective-permute-start.38 = (bf16[64,1536]{1,0:T(8,128)(2,1)S(1)}, bf16[64,1536]{1,0:T(8,128)(2,1)S(1)}, u32[]{:S(2)}, u32[]{:S(2)}) collective-permute-start(bf16[64,1536]{1,0:T(8,128)(2,1)S(1)} %select_convert_fusion.1), channel_id=1, source_target_pairs={{0,16},{2,18},{4,20},{6,22},{8,24},{10,26},{12,28},{14,30},{16,0},... | collective-permute-start | bytes 589832 | tf_op jit(solution)/shard_map/ppermute | solution.py:14
  293.7 17.1 %collective-permute-start.41 = (bf16[64,1536]{1,0:T(8,128)(2,1)S(1)}, bf16[64,1536]{1,0:T(8,128)(2,1)S(1)}, u32[]{:S(2)}, u32[]{:S(2)}) collective-permute-start(bf16[64,1536]{1,0:T(8,128)(2,1)S(1)} %convert_add_fusion.1), channel_id=1, source_target_pairs={{0,2},{2,0},{4,6},{6,4},{8,10},{10,8},{12,14},{14,12},{16,18},{18,... | collective-permute-start | bytes 589832 | tf_op jit(solution)/shard_map/ppermute | solution.py:14
  295.1 23.0 %collective-permute-start.39 = (bf16[256,2048]{1,0:T(8,128)(2,1)}, bf16[256,2048]{1,0:T(8,128)(2,1)}, u32[]{:S(2)}, u32[]{:S(2)}) collective-permute-start(bf16[256,2048]{1,0:T(8,128)(2,1)} %collective-permute-done.36.refs_6_.refs_2_), channel_id=1, source_target_pairs={{16,24},{18,26},{20,28},{22,30},{17,25},{19,27},{21,29},{23,31}} | collective-permute-start | bytes 3145736 | tf_op jit(solution)/shard_map/ppermute | solution.py:263
  296.7 25.8 %collective-permute-start.40 = (bf16[256,2048]{1,0:T(8,128)(2,1)S(1)}, bf16[256,2048]{1,0:T(8,128)(2,1)}, u32[]{:S(2)}, u32[]{:S(2)}) collective-permute-start(bf16[256,2048]{1,0:T(8,128)(2,1)S(1)} %copy-done.18), channel_id=1, source_target_pairs={{8,0},{10,2},{12,4},{14,6},{9,1},{11,3},{13,5},{15,7}} | collective-permute-start | bytes 3145736 | tf_op jit(solution)/shard_map/ppermute | solution.py:268
  298.0 24.5 %collective-permute-start.33 = (bf16[512,1024]{1,0:T(8,128)(2,1)}, bf16[512,1024]{1,0:T(8,128)(2,1)S(1)}, u32[]{:S(2)}, u32[]{:S(2)}) collective-permute-start(bf16[512,1024]{1,0:T(8,128)(2,1)} %pad_maximum_fusion.2), channel_id=1, source_target_pairs={{0,4},{2,6},{4,0},{6,2},{8,12},{10,14},{12,8},{14,10},{16,20},{18,... | collective-permute-start | bytes 3145736 | tf_op jit(solution)/shard_map/ppermute | solution.py:389
  299.6 23.9 %collective-permute-start.34 = (bf16[512,1024]{1,0:T(8,128)(2,1)}, bf16[512,1024]{1,0:T(8,128)(2,1)}, u32[]{:S(2)}, u32[]{:S(2)}) collective-permute-start(bf16[512,1024]{1,0:T(8,128)(2,1)} %pad_maximum_fusion.3), channel_id=1, source_target_pairs={{0,2},{2,0},{4,6},{6,4},{8,10},{10,8},{12,14},{14,12},{16,18},{18,... | collective-permute-start | bytes 3145736 | tf_op jit(solution)/shard_map/ppermute | solution.py:388
  326.5 7.3 %collective-permute-start.46 = (bf16[64,1536]{1,0:T(8,128)(2,1)S(1)}, bf16[64,1536]{1,0:T(8,128)(2,1)S(1)}, u32[]{:S(2)}, u32[]{:S(2)}) collective-permute-start(bf16[64,1536]{1,0:T(8,128)(2,1)S(1)} %add_convert_fusion.1), channel_id=1, source_target_pairs={{0,4},{2,6},{4,0},{6,2},{8,12},{10,14},{12,8},{14,10},{16,20},{18,... | collective-permute-start | bytes 589832 | tf_op jit(solution)/shard_map/ppermute | solution.py:14
  330.5 13.0 %collective-permute-start.43 = (bf16[256,1024]{1,0:T(8,128)(2,1)S(1)}, bf16[256,1024]{1,0:T(8,128)(2,1)S(1)}, u32[]{:S(2)}, u32[]{:S(2)}) collective-permute-start(bf16[256,1024]{1,0:T(8,128)(2,1)S(1)} %slice.355), channel_id=1, source_target_pairs={{0,4},{2,6},{4,0},{6,2},{8,12},{10,14},{12,8},{14,10},{16,20},{18,... | collective-permute-start | bytes 1572872 | tf_op jit(solution)/shard_map/ppermute | solution.py:389
  331.8 11.7 %collective-permute-start.44 = (bf16[256,1024]{1,0:T(8,128)(2,1)S(1)}, bf16[256,1024]{1,0:T(8,128)(2,1)S(1)}, u32[]{:S(2)}, u32[]{:S(2)}) collective-permute-start(bf16[256,1024]{1,0:T(8,128)(2,1)S(1)} %slice.356), channel_id=1, source_target_pairs={{0,2},{2,0},{4,6},{6,4},{8,10},{10,8},{12,14},{14,12},{16,18},{18,... | collective-permute-start | bytes 1572872 | tf_op jit(solution)/shard_map/ppermute | solution.py:388
  333.8 7.8 %collective-permute-start.47 = (bf16[64,1536]{1,0:T(8,128)(2,1)S(1)}, bf16[64,1536]{1,0:T(8,128)(2,1)S(1)}, u32[]{:S(2)}, u32[]{:S(2)}) collective-permute-start(bf16[64,1536]{1,0:T(8,128)(2,1)S(1)} %add_convert_fusion), channel_id=1, source_target_pairs={{0,16},{2,18},{4,20},{6,22},{8,24},{10,26},{12,28},{14,30},{16,0},... | collective-permute-start | bytes 589832 | tf_op jit(solution)/shard_map/ppermute | solution.py:14
  339.7 10.1 %collective-permute-start.42 = (bf16[512,512]{1,0:T(8,128)(2,1)S(1)}, bf16[512,512]{1,0:T(8,128)(2,1)S(1)}, u32[]{:S(2)}, u32[]{:S(2)}) collective-permute-start(bf16[512,512]{1,0:T(8,128)(2,1)S(1)} %fusion.14.refs_0_), channel_id=1, source_target_pairs={{0,1},{1,0},{2,3},{3,2},{4,5},{5,4},{6,7},{7,6},{8,9},{9,8},{10,11... | collective-permute-start | bytes 1572872 | tf_op jit(solution)/shard_map/ppermute | solution.py:304
  347.3 24.5 %collective-permute-start.48 = (bf16[64,3072]{1,0:T(8,128)(2,1)}, bf16[64,3072]{1,0:T(8,128)(2,1)}, u32[]{:S(2)}, u32[]{:S(2)}) collective-permute-start(bf16[64,3072]{1,0:T(8,128)(2,1)} %pad_maximum_fusion.7), channel_id=1, source_target_pairs={{0,8},{2,10},{4,12},{6,14},{8,0},{10,2},{12,4},{14,6},{16,24},{18,... | collective-permute-start | bytes 1179656 | tf_op jit(solution)/shard_map/ppermute | solution.py:14
  353.5 39.0 %collective-permute-start.53 = (f32[64,4096]{1,0:T(8,128)}, f32[64,4096]{1,0:T(8,128)S(1)}, u32[]{:S(2)}, u32[]{:S(2)}) collective-permute-start(f32[64,4096]{1,0:T(8,128)} %fusion.18), channel_id=1, source_target_pairs={{0,1},{1,0},{2,3},{3,2},{4,5},{5,4},{6,7},{7,6},{8,9},{9,8},{10,11... | collective-permute-start | bytes 3145736 | tf_op jit(solution)/shard_map/ppermute | solution.py:304
  355.2 16.3 %collective-permute-start.50 = (f32[4096]{0:T(1024)S(1)}, f32[4096]{0:T(1024)S(1)}, u32[]{:S(2)}, u32[]{:S(2)}) collective-permute-start(f32[4096]{0:T(1024)S(1)} %add.257), channel_id=1, source_target_pairs={{0,4},{2,6},{4,0},{6,2},{8,12},{10,14},{12,8},{14,10},{16,20},{18,... | collective-permute-start | bytes 49160 | tf_op jit(solution)/shard_map/ppermute | solution.py:14
  375.4 6.6 %collective-permute-start.52 = (f32[4096]{0:T(1024)S(1)}, f32[4096]{0:T(1024)S(1)}, u32[]{:S(2)}, u32[]{:S(2)}) collective-permute-start(f32[4096]{0:T(1024)S(1)} %add.259), channel_id=1, source_target_pairs={{0,16},{2,18},{4,20},{6,22},{8,24},{10,26},{12,28},{14,30},{16,0},... | collective-permute-start | bytes 49160 | tf_op jit(solution)/shard_map/ppermute | solution.py:14
  (93 other events, 708.6 us)
Sparse Core Ops, SparseCore 0:
  23.3 10.8 all-gather.1
